TPU v7x, 128 devices: a whole 4x4x4 slice. The times are simulated.
128 devices in a mesh: dp: 8 (over z, y_lo), tensor: 16 (over x, y_hi, core).
Axes of the slice: x: 4, y: 4 (y_hi: 2, y_lo: 2; y = y_hi * 2 + y_lo), z: 4, core: 2. Of those that a mesh axis runs over, the one named last changes fastest.
Arguments:
- doc_inputs: bfloat16 [4096, 8192], P('dp'), may hold values from -6 to 6
- doc_hidden_grads: bfloat16 [4096, 14336], P('dp', 'tensor'), may hold values from -6 to 6
- query_inputs: bfloat16 [2048, 8192], P('dp'), may hold values from -6 to 6
- query_hidden_grads: bfloat16 [2048, 14336], P('dp', 'tensor'), may hold values from -6 to 6
- gate_weight: bfloat16 [8192, 14336], P('dp', 'tensor'), may hold values from -0.0625 to 0.0625
- up_weight: bfloat16 [8192, 14336], P('dp', 'tensor'), may hold values from -0.0625 to 0.0625
- doc_ids: int32 [8, 512], P('dp'), may hold values from 0 to 3, never falling along the last dimension, each value on 1 to 256 neighbouring positions
- query_ids: int32 [8, 256], replicated, may hold values from 0 to 3, never falling along the last dimension, each value on 1 to 128 neighbouring positions
Outputs:
- scores: float32 [8, 4, 32], P('dp')
Inputs may be any that keep to these rules, and one draw needn't show every extreme that they name: `doc_ids`: within each row the ids never fall, every id 0 to 3 occurs, and one document has exactly 256 tokens. `query_ids`: within each row the ids never fall, every id 0 to 3 occurs, and one query has exactly 128 tokens.
All inputs are finite; a program needn't handle non-finite values.
Results may differ from a plain program's by a relative error of at most 0.0039.
Values may be sent and summed in bfloat16 or wider, within the bound.
No kernel may reach another device: no remote copies, remote signals or barrier semaphores. Data moves between devices by JAX's collectives and lax.ppermute only.
A program may use at most 192 MiB of HBM per device.

v0:
```python
import functools
import math

import jax
import jax.numpy as jnp
from jax import lax
from jax.experimental import pallas as pl
from jax.experimental.pallas import tpu as pltpu
from jax.sharding import PartitionSpec as P

D = 8192
FF = 14336
DOCS = 4
QS = 4
TOK = 512
QTOK = 256
ROWS = TOK + QTOK
BLK = D // 8
THIN = BLK + 512
AX = ("dp", "tensor")
F32 = jnp.float32
BF16 = jnp.bfloat16


def place(z, y, x, c):
    return ((z % 4) * 2 + (y % 2)) * 16 + (x % 4) * 4 + ((y % 4) // 2) * 2 + c


def perm(fn):
    return [
        (place(z, y, x, c), place(*fn(z, y, x, c)))
        for z in range(4)
        for y in range(4)
        for x in range(4)
        for c in range(2)
    ]


ZP = perm(lambda z, y, x, c: (z + 1, y, x, c))
ZM = perm(lambda z, y, x, c: (z - 1, y, x, c))
XP = perm(lambda z, y, x, c: (z, y, x + 1, c))
XM = perm(lambda z, y, x, c: (z, y, x - 1, c))
PARTNER = perm(lambda z, y, x, c: (z, y ^ 1, x, c))
OTHER = perm(lambda z, y, x, c: (z, (3 - y) % 4, x, c))
CORE = perm(lambda z, y, x, c: (z, y, x, 1 - c))
X1 = perm(lambda z, y, x, c: (z, y, x ^ 1, c))
X3 = perm(lambda z, y, x, c: (z, y, 3 - x, c))
STEPS = (0, -1, 1, 2)
LIMIT = 56 << 20
SLOTS = 3
SMALL = pl.CostEstimate(flops=1 << 10, bytes_accessed=1 << 10, transcendentals=0)
PLANES = [[place(z, y, x, c) for x in range(4) for y in range(4) for c in range(2)] for z in range(4)]
ZGROUPS = [[place(z, y, x, c) for z in range(4)] for y in range(4) for x in range(4) for c in range(2)]
NT = (((1,), (1,)), ((), ()))


def send(v, p):
    return lax.ppermute(v, AX, p)


def tie(*vs):
    return lax.optimization_barrier(vs)


def columns_of(half, gate, up, wide, thin, thin_rows):
    gh, uh = gate[:, 384:512].astype(F32), up[:, 384:512].astype(F32)
    low = lax.broadcasted_iota(jnp.int32, gh.shape, 1) < 64
    first = jnp.where(low, gh, pltpu.roll(uh, 64, 1))
    second = jnp.where(low, pltpu.roll(gh, 64, 1), uh)
    base = pl.multiple_of(half * 512, 128)
    wide[:, :256] = gate[:, pl.ds(base, 256)]
    wide[:, 256:512] = up[:, pl.ds(base, 256)]
    wide[:, 512:] = jnp.where(half == 0, first, second).astype(BF16)
    base = pl.multiple_of(half * 512 + 256, 128)
    thin[thin_rows, :128] = gate[:, pl.ds(base, 128)]
    thin[thin_rows, 128:] = up[:, pl.ds(base, 128)]


def pack_kernel(s, gate, up, doc, query, some, keep0, keep1, give0, give1, piece):
    i = pl.program_id(0)
    columns_of(s[0], gate, up, keep0, keep1, pl.ds(i * gate.shape[0], gate.shape[0]))
    columns_of(1 - s[0], gate, up, give0, give1, slice(None))
    piece[pl.ds(i * doc.shape[0], doc.shape[0])] = doc[...]
    piece[pl.ds(TOK + i * query.shape[0], query.shape[0])] = query[...]

    @pl.when(i == 0)
    def _():
        for j in range(32):
            keep1[BLK + 16 * j : BLK + 16 * j + 16] = some[:, 256 * j : 256 * j + 256]


def pack(scalars, gate, up, doc, query):
    steps = 2
    rows = BLK // steps
    spec = lambda n: pl.BlockSpec((rows, n), lambda i, s: (i, 0))
    whole = lambda *shape: pl.BlockSpec(shape, lambda i, s: (0, 0))
    shape = lambda r, n: jax.ShapeDtypeStruct((r, n), BF16)
    column = lambda n: pl.BlockSpec((n // steps, BLK), lambda i, s: (i, s[1]))
    return pl.pallas_call(
        pack_kernel,
        grid_spec=pltpu.PrefetchScalarGridSpec(
            num_scalar_prefetch=1,
            grid=(steps,),
            in_specs=[spec(896), spec(896), column(TOK), column(QTOK), pl.BlockSpec((16, D), lambda i, s: (s[2], 0))],
            out_specs=[spec(640), whole(THIN, 256), spec(640), spec(256), whole(ROWS, BLK)],
        ),
        out_shape=[shape(BLK, 640), shape(THIN, 256), shape(BLK, 640), shape(BLK, 256), shape(ROWS, BLK)],
        compiler_params=pltpu.CompilerParams(vmem_limit_bytes=LIMIT),
        cost_estimate=SMALL,
    )(scalars, gate, up, doc, query, query)


def pack_grads_kernel(ylo_ref, doc, query, ids, keep, give):
    ylo = ylo_ref[0]
    give[ROWS:] = jnp.broadcast_to(ids[...].astype(F32), (16, TOK)).astype(BF16)
    for src, lo, n in ((doc, 0, TOK), (query, TOK, QTOK)):
        h = src[:, 384:512].astype(F32)
        t = pltpu.roll(h, 64, 1)
        low = lax.broadcasted_iota(jnp.int32, h.shape, 1) < 64
        first, second = jnp.where(low, h, t), jnp.where(low, t, h)
        for s, out in ((ylo, keep), (1 - ylo, give)):
            out[lo : lo + n, :384] = src[:, pl.ds(pl.multiple_of(s * 512, 128), 384)]
            out[lo : lo + n, 384:] = jnp.where(s == 0, first, second).astype(BF16)


def pack_grads(ylo, doc, query, ids):
    vmem = pl.BlockSpec(memory_space=pltpu.VMEM)
    return pl.pallas_call(
        pack_grads_kernel,
        in_specs=[pl.BlockSpec(memory_space=pltpu.SMEM), vmem, vmem, vmem],
        out_specs=[vmem, vmem],
        out_shape=[jax.ShapeDtypeStruct((ROWS, 512), BF16), jax.ShapeDtypeStruct((ROWS + 16, 512), BF16)],
        compiler_params=pltpu.CompilerParams(vmem_limit_bytes=LIMIT),
        cost_estimate=SMALL,
    )(ylo, doc, query, ids)


def halves_a_kernel(below, above, far0, far1):
    far0[0] = below[...]
    far1[0] = above[...]


def halves_b_kernel(below, above, x_below, x_above, _0, _1, far0, far1, x_far0, x_far1):
    far0[0] = below[...]
    far1[0] = above[...]
    x_far0[...] = x_below[...]
    x_far1[...] = x_above[...]


def halves(below, above, x=(), into=()):
    steps = 2
    spec = lambda rows, n, at: pl.BlockSpec((rows // steps, n), lambda i: (at * steps + i, 0))
    n, m = BLK // 2, ROWS // 2
    which = 1 if into else 0
    out_specs = [pl.BlockSpec((1, n // steps, 640), lambda i: (which, i, 0))] * 2
    out_shape = [jax.ShapeDtypeStruct((2, n, 640), BF16)] * 2
    in_specs = [spec(n, 640, 0), spec(n, 640, 1)]
    if into:
        in_specs += [spec(m, BLK, 0), spec(m, BLK, 1)] + [pl.BlockSpec(memory_space=pl.ANY)] * 2
        out_specs += [spec(m, BLK, 0)] * 2
        out_shape += [jax.ShapeDtypeStruct((m, BLK), BF16)] * 2
    return pl.pallas_call(
        halves_b_kernel if into else halves_a_kernel,
        grid=(steps,),
        in_specs=in_specs,
        out_specs=out_specs,
        out_shape=out_shape,
        input_output_aliases={4: 0, 5: 1} if into else {},
        compiler_params=pltpu.CompilerParams(vmem_limit_bytes=LIMIT),
        cost_estimate=SMALL,
    )(below, above, *x, *into)


def gated(hidden, gate, up):
    s = jax.nn.sigmoid(gate)
    up_factor = (hidden * gate * s).astype(BF16)
    gate_factor = (hidden * up * s * (1.0 + gate * (1.0 - s))).astype(BF16)
    return gate_factor, up_factor


def factor_kernel(phases, m, row, nw, nt, nx, s, *refs):
    def take(n):
        nonlocal refs
        got, refs = refs[:n], refs[n:]
        return got

    ends = phases[0][3]
    ws, thins, own_x, other_x = take(nw), take(nt), take(2), take(nx)
    befores = [None if begins else take(1)[0] for _, _, begins, _ in phases]
    hidden = [take(1)[0] for _ in phases] if ends else None
    outs = take(1 if ends else len(phases))
    acc, wv, xv, wsem, xsem, bsem, osem = refs[:7]
    hv, hsem = refs[7:] if ends else (None, None)
    steps = [(p, k) for p, phase in enumerate(phases) for k in range(phase[1])]
    half = ROWS // 2

    def start(g):
        p, k = steps[g]
        at = g % SLOTS
        base = 32 * p
        block = s[base + k]
        for w in range(nw):

            @pl.when(s[base + 16 + k] == w)
            def _():
                if w < 6:
                    pltpu.make_async_copy(ws[w], wv.at[at, :, pl.ds(0, 640)], wsem.at[at]).start()
                else:
                    n = BLK // 2
                    rows = pl.ds((w - 6) * n, n)
                    for part in (0, 1):
                        pltpu.make_async_copy(
                            ws[6 + part].at[rows], wv.at[at, pl.ds(part * n, n), pl.ds(0, 640)], wsem.at[at]
                        ).start()

        for flip in range(nt):
            rows = pl.ds(pl.multiple_of(block // 2 * (BLK if flip else THIN), 512), BLK)

            @pl.when(lax.rem(block, 2) == (s[base + 24] ^ flip))
            def _():
                pltpu.make_async_copy(thins[flip].at[rows], wv.at[at, :, pl.ds(640, 256)], wsem.at[at]).start()

        if phases[p][0] == "own":
            cols = pl.ds(pl.multiple_of(block * BLK, BLK), BLK)
            for x, lo, n in ((own_x[0], 0, TOK), (own_x[1], TOK, QTOK)):
                if row <= lo < row + m:
                    pltpu.make_async_copy(x.at[:, cols], xv.at[at, pl.ds(lo - row, n)], xsem.at[at]).start()
        else:
            for q in range(min(nx, 8)):

                @pl.when(s[base + 8 + k] == q)
                def _():
                    if q < 6:
                        pltpu.make_async_copy(other_x[q].at[pl.ds(row, m)], xv.at[at], xsem.at[at]).start()
                    else:
                        for part in (0, 1):
                            lo = max(row, part * half)
                            hi = min(row + m, part * half + half)
                            if lo < hi:
                                pltpu.make_async_copy(
                                    other_x[6 + (q - 6) * 2 + part].at[pl.ds(lo - part * half, hi - lo)],
                                    xv.at[at, pl.ds(lo - row, hi - lo)],
                                    xsem.at[at],
                                ).start()

    def load(p):
        if befores[p] is not None:
            pltpu.make_async_copy(befores[p].at[pl.ds(row, m)], acc.at[p], bsem.at[p]).start()

    def finish(p):
        hidden_copy(p).wait()
        dst, to = outs[0], slice(p * m, p * m + m)
        g, u = gated(hv[p, :, :256].astype(F32), acc[p, :, :256], acc[p, :, 256:512])
        dst[to, :256] = g
        dst[to, 256:512] = u
        both = acc[p, :, 512:640]
        turned = pltpu.roll(both, 64, 1)
        low = lax.broadcasted_iota(jnp.int32, both.shape, 1) < 64
        g, u = gated(hv[p, :, 384:].astype(F32), jnp.where(low, both, turned), jnp.where(low, turned, both))
        dst[to, 512:640] = jnp.where(low, g.astype(F32), u.astype(F32)).astype(BF16)
        g, u = gated(hv[p, :, 256:384].astype(F32), acc[p, :, 640:768], acc[p, :, 768:])
        dst[to, 640:768] = g
        dst[to, 768:] = u

    hidden_copy = lambda p: pltpu.make_async_copy(hidden[p].at[pl.ds(row, m)], hv.at[p], hsem.at[p])
    out_copy = lambda p: pltpu.make_async_copy(acc.at[p], outs[p], osem.at[p])
    i = pl.program_id(0)
    slot = lax.rem(i, SLOTS)
    firsts = [sum(phase[1] for phase in phases[:p]) for p in range(len(phases) + 1)]

    @pl.when(i == 0)
    def _():
        start(0)
        load(0)

    for v, sem in ((wv, wsem), (xv, xsem)):
        pltpu.make_async_copy(v.at[slot], v.at[slot], sem.at[slot]).wait()

    for g in range(1, len(steps)):

        @pl.when(i == max(g - (SLOTS - 1), 0))
        def _():
            start(g)

    @pl.when(i == 0)
    def _():
        for p in range(1, len(phases)):
            load(p)
        if ends:
            for p in range(len(phases)):
                hidden_copy(p).start()

    for p in range(len(phases)):

        @pl.when(i == firsts[p])
        def _():
            if befores[p] is None:
                acc[p] = jnp.zeros((m, 896), F32)
            else:
                pltpu.make_async_copy(befores[p].at[pl.ds(row, m)], acc.at[p], bsem.at[p]).wait()

    now = jnp.where(i >= firsts[1], 1, 0) if len(phases) > 1 else 0
    acc[now] += jnp.dot(xv[slot], wv[slot], preferred_element_type=F32)

    for p in range(len(phases)):

        @pl.when(i == firsts[p + 1] - 1)
        def _():
            if ends:
                finish(p)
            else:
                out_copy(p).start()

    if not ends:

        @pl.when(i == len(steps) - 1)
        def _():
            for p in range(len(phases)):
                out_copy(p).wait()


def factors(phases, scalars, ws, thins, own, other=(), befores=(), hidden=(), rows=(0, ROWS)):
    row, m = rows
    ends = phases[0][3]
    hbm = pl.BlockSpec(memory_space=pl.ANY)
    whole = lambda v: pl.BlockSpec(v.shape, lambda i, s: (0, 0))
    args = [*ws, *thins, *own, *other, *befores, *hidden]
    in_specs = [hbm] * len(args)
    if ends:
        out_shape = [jax.ShapeDtypeStruct((len(phases) * m, 896), BF16)]
        out_specs = [whole(out_shape[0])]
    else:
        out_shape = [jax.ShapeDtypeStruct((m, 896), F32)] * len(phases)
        out_specs = [hbm] * len(phases)
    return pl.pallas_call(
        functools.partial(factor_kernel, phases, m, row, len(ws), len(thins), len(other)),
        grid_spec=pltpu.PrefetchScalarGridSpec(
            num_scalar_prefetch=1,
            grid=(sum(phase[1] for phase in phases),),
            in_specs=in_specs,
            out_specs=out_specs,
            scratch_shapes=[
                pltpu.VMEM((len(phases), m, 896), F32),
                pltpu.VMEM((SLOTS, BLK, 896), BF16),
                pltpu.VMEM((SLOTS, m, BLK), BF16),
                pltpu.SemaphoreType.DMA((SLOTS,)),
                pltpu.SemaphoreType.DMA((SLOTS,)),
                pltpu.SemaphoreType.DMA((len(phases),)),
                pltpu.SemaphoreType.DMA((len(phases),)),
            ]
            + ([pltpu.VMEM((len(phases), m, 512), BF16), pltpu.SemaphoreType.DMA((len(phases),))] if ends else []),
        ),
        out_shape=out_shape,
        compiler_params=pltpu.CompilerParams(vmem_limit_bytes=LIMIT),
        cost_estimate=SMALL,
    )(scalars, *args)


def unpack_kernel(thin, few):
    for z in range(4):
        for j in range(32):
            lo = 16 * j
            few[16 * z : 16 * z + 16, 256 * j : 256 * j + 256] = thin[z, lo : lo + 16]


def unpack(thin):
    return pl.pallas_call(
        unpack_kernel,
        grid=(1,),
        in_specs=[pl.BlockSpec((4, 512, 256), lambda k: (0, 2, 0))],
        out_specs=pl.BlockSpec((64, D), lambda k: (0, 0)),
        out_shape=jax.ShapeDtypeStruct((64, D), BF16),
        compiler_params=pltpu.CompilerParams(vmem_limit_bytes=LIMIT),
        cost_estimate=SMALL,
    )(thin.reshape(4, THIN, 256))


def gram_kernel(mine, theirs, doc, out, acc):
    k = pl.program_id(0)

    @pl.when(k == 0)
    def _():
        acc[...] = jnp.zeros_like(acc)

    few = jnp.concatenate([mine[...], theirs[...]], 0)
    acc[...] += lax.dot_general(doc[...], few, NT, preferred_element_type=F32)

    @pl.when(k == 7)
    def _():
        out[...] = acc[...].T.astype(BF16)


def gram_part(mine, theirs, doc):
    few = pl.BlockSpec((64, BLK), lambda k: (0, k))
    return pl.pallas_call(
        gram_kernel,
        grid=(8,),
        in_specs=[few, few, pl.BlockSpec((TOK, BLK), lambda k: (0, k))],
        out_specs=pl.BlockSpec((128, TOK), lambda k: (0, 0)),
        scratch_shapes=[pltpu.VMEM((TOK, 128), F32)],
        out_shape=jax.ShapeDtypeStruct((128, TOK), BF16),
        compiler_params=pltpu.CompilerParams(vmem_limit_bytes=LIMIT),
        cost_estimate=SMALL,
    )(mine, theirs, doc)


def hop(r):
    return jnp.where(r == 0, 0, jnp.where(r == 1, 3, jnp.where(r == 2, 1, 2)))


def score_kernel(first, count, s, *refs):
    qs, (d, gram, ids, docs, before, out, f, b, acc) = refs[:count], refs[count:]
    i = pl.program_id(0)
    r = first + i
    z, ylo = s[0], s[1]

    @pl.when(i == 0)
    def _():
        acc[...] = jnp.zeros_like(acc)

    if first == 3:
        f[:QTOK] = qs[0][...]
        f[QTOK:] = qs[1][...]
    else:
        for n in range(count):

            @pl.when(i == n)
            def _():
                f[...] = qs[n][...]

    for flip in (0, 1):
        b[...] = lax.dot_general(f[flip * QTOK : flip * QTOK + QTOK], d[...], NT, preferred_element_type=F32)
        sums = [[jnp.zeros((8, TOK), F32) for _ in range(QS)] for _ in (0, 1)]
        for y in range(4):
            whose = ylo ^ (y % 2)
            docs_at = pl.ds(pl.multiple_of(whose * TOK, TOK), TOK)
            for x in range(4):
                for core in range(2):
                    lo = x * 64 + y // 2 * 32 + core * 16
                    p = gram[x, y, core, whose ^ flip, 0].astype(F32) * b[lo : lo + 16, docs_at]
                    who = ids[flip * QTOK + lo : flip * QTOK + lo + 16, :]
                    for k in range(QS):
                        t = jnp.where(who == k, p, 0.0)
                        sums[y % 2][k] = sums[y % 2][k] + (t[:8] + t[8:])
        group = lax.rem(z + hop(r), 4) * 2 + (ylo ^ flip)
        for k in range(QS):
            for y in (0, 1):
                at = slice(y * TOK, y * TOK + TOK)
                acc[pl.ds(group * QS + k, 1), at] = jnp.sum(sums[y][k], 0, keepdims=True)

    @pl.when(i == pl.num_programs(0) - 1)
    def _():
        for k in range(2 * DOCS):
            at = slice(k // DOCS * TOK, k // DOCS * TOK + TOK)
            out[:, k : k + 1] = before[:, k : k + 1] + jnp.sum(acc[:, at] * docs[k : k + 1, at], 1, keepdims=True)


def score_sums(first, scalars, queries, documents, gram, ids, docs, before):
    whole = lambda v: pl.BlockSpec(v.shape, lambda r, s: (0, 0))
    planes = pl.BlockSpec((4, 4, 2, 2, 1, 16, TOK), lambda r, s: (0, 0, 0, 0, lax.rem(s[0] + hop(first + r), 4), 0, 0))
    return pl.pallas_call(
        functools.partial(score_kernel, first, len(queries)),
        grid_spec=pltpu.PrefetchScalarGridSpec(
            num_scalar_prefetch=1,
            grid=(1 if first == 3 else len(queries),),
            in_specs=[whole(v) for v in (*queries, documents)]
            + [planes, pl.BlockSpec((2 * QTOK, 1), lambda r, s: (first + r, 0)), whole(docs), whole(before)],
            out_specs=whole(before),
            scratch_shapes=[
                pltpu.VMEM((2 * QTOK, 896), BF16),
                pltpu.VMEM((QTOK, 2 * TOK), F32),
                pltpu.VMEM((8 * QS, 2 * TOK), F32),
            ],
        ),
        out_shape=jax.ShapeDtypeStruct(before.shape, F32),
        compiler_params=pltpu.CompilerParams(vmem_limit_bytes=24 << 20),
        cost_estimate=SMALL,
    )(scalars, *queries, documents, gram, ids, docs, before)


def local(doc_inputs, doc_grads, query_inputs, query_grads, gate_weight, up_weight, doc_ids, query_ids):
    dp = lax.axis_index("dp")
    tensor = lax.axis_index("tensor")
    z, ylo = dp // 2, dp % 2
    x, core = tensor // 4, tensor % 2
    ints = lambda *vs: jnp.stack([jnp.asarray(v, jnp.int32) for v in vs])

    def scalars(blocks):
        blocks = ints(*blocks)
        turn = (blocks // 2 - x + 4) % 4
        at = jnp.where(turn == 0, 0, jnp.where(turn == 3, 1, jnp.where(turn == 1, 2, 3)))
        which_x = at * 2 + ((blocks % 2) ^ core)
        turn = (blocks // 2 - z + 4) % 4
        flip = (blocks % 2) ^ ylo
        which_w = jnp.where(
            turn == 2, 6 + flip, flip * 3 + jnp.where(turn == 0, 0, jnp.where(turn == 3, 1, 2))
        )
        spare = jnp.zeros((8 - blocks.shape[0],), jnp.int32)
        last = jnp.full((8,), ylo)
        return jnp.concatenate([blocks, spare, which_x, spare, which_w, spare, last]).astype(jnp.int32)

    first = scalars([(z + dz + 4) % 4 * 2 + ylo for dz in (0, -1, 1)])
    second = scalars([(z + dz + 4) % 4 * 2 + (ylo ^ 1) for dz in (0, -1, 1)])
    last = scalars([(z + 2) % 4 * 2 + flip for flip in (0, 1)])
    late = (z + 2) % 4, jnp.where(x == z, (z + 3) % 4, (x + 2) % 4)
    free = [jnp.logical_and(late[0] != v, late[1] != v) for v in range(4)]
    soon = jnp.where(free[0], 0, jnp.where(free[1], 1, 2)), jnp.where(free[3], 3, jnp.where(free[2], 2, 1))
    blocks_of = lambda zs: [v * 2 + flip for v in zs for flip in (0, 1)]
    early = jnp.concatenate([second, scalars(blocks_of(soon))])
    late = jnp.concatenate([last, scalars(blocks_of(late))])
    where = ints(z, ylo)

    keep0, keep1, give0, give1, piece = pack(
        ints(ylo, x * 2 + core, tensor), gate_weight, up_weight, doc_inputs, query_inputs
    )
    thin_a = lax.all_gather(keep1, AX, axis_index_groups=ZGROUPS, axis=0, tiled=True)
    a_below, a_above = send(keep0, ZP), send(keep0, ZM)
    got0 = send(give0, PARTNER)
    piece = send(piece, OTHER)
    got1 = send(give1, PARTNER)
    mine, theirs = pack_grads(ints(ylo), doc_grads, query_grads, doc_ids)
    order = jnp.stack([(z + dz + 4) % 4 * 2 + (ylo ^ flip) for dz in STEPS for flip in (0, 1)])
    ids = query_ids[order].reshape(-1, 1)
    got0, piece, a_below, a_above, got1, ids, first, early, late, where, mine, theirs = tie(
        got0, piece, a_below, a_above, got1, ids, first, early, late, where, mine, theirs
    )
    thin_b = lax.all_gather(got1, AX, axis_index_groups=ZGROUPS, axis=0, tiled=True)
    b_below, b_above = send(got0, ZP), send(got0, ZM)
    x_below, x_above = send(piece, XP), send(piece, XM)
    own = (doc_inputs, query_inputs)
    a_w = [keep0, a_below, a_above]
    (own_part,) = factors((("own", 3, True, False),), first, a_w, [thin_a], own)
    few = unpack(thin_a)
    few_too = send(few, PARTNER)
    few_too, theirs = tie(few_too, theirs)
    gram = gram_part(few, few_too, doc_inputs)
    theirs = send(theirs, PARTNER)
    into = halves(a_below, a_above)
    b_below, b_above, x_below, x_above, piece, own_part, gram, *into = tie(
        b_below, b_above, x_below, x_above, piece, own_part, gram, *into
    )
    thins = [thin_a, thin_b]
    far0, far1, x_far0, x_far1 = halves(b_below, b_above, (x_below, x_above), into)
    far0, far1 = send(far0.reshape(BLK, 640), ZP), send(far1.reshape(BLK, 640), ZM)
    piece_too, x_below_too, x_above_too = send(piece, CORE), send(x_below, CORE), send(x_above, CORE)
    piece_too, x_below_too, x_above_too, x_far0, x_far1 = tie(piece_too, x_below_too, x_above_too, x_far0, x_far1)
    x_far0, x_far1 = send(x_far0, XP), send(x_far1, XM)
    near_x = [piece, piece_too, x_below, x_below_too, x_above, x_above_too]
    near_w = [*a_w, got0, b_below, b_above]
    own_part, other_part = factors(
        (("own", 3, False, False), ("other", 4, True, False)), early, near_w, thins, own, near_x, [own_part]
    )
    gram = lax.all_gather(gram, AX, axis_index_groups=PLANES, axis=0, tiled=True).reshape(4, 4, 2, 2, 4, 16, TOK)
    x_far0, x_far1, far0, far1, own_part, other_part, theirs = tie(
        x_far0, x_far1, far0, far1, own_part, other_part, theirs
    )
    all_w = [*near_w, far0, far1]
    all_x = [*near_x, x_far0, x_far1, send(x_far0, CORE), send(x_far1, CORE)]

    rest = (("own", 2, False, True), ("other", 4, False, True))
    parts, grads = (own_part, other_part), (mine, theirs)
    (q,) = factors(rest, late, all_w, thins, own, all_x, parts, grads, (TOK, QTOK))
    q, own_part, ids_too = tie(q, own_part, theirs[ROWS : ROWS + 1])
    ids_too = ids_too.astype(jnp.int32)
    lower, upper = jnp.where(ylo == 0, doc_ids, ids_too), jnp.where(ylo == 0, ids_too, doc_ids)
    both = jnp.concatenate([lower, upper + DOCS], 1)
    docs = (both == jnp.arange(2 * DOCS, dtype=jnp.int32)[:, None]).astype(F32)
    q_below, q_above = send(q, ZP), send(q, ZM)
    (d,) = factors(rest, late, all_w, thins, own, all_x, (own_part, other_part), grads, (0, TOK))
    q_below, q_above, d = tie(q_below, q_above, d)
    q_far0, q_far1 = send(q_below[:QTOK], ZP), send(q_above[QTOK:], ZM)

    scores = jnp.zeros((8 * QS, 2 * DOCS), F32)
    scores = score_sums(0, where, (q, q_below, q_above), d, gram, ids, docs, scores)
    scores = score_sums(3, where, (q_far0, q_far1), d, gram, ids, docs, scores)

    for p in (CORE, X1, X3, PARTNER, OTHER):
        scores = scores + send(scores, p)
    scores = jnp.where(ylo == 0, scores[:, :DOCS], scores[:, DOCS:]).T / math.sqrt(D * FF)
    return scores[None]


def solution(mesh):
    placed = (
        P("dp", None),
        P("dp", "tensor"),
        P("dp", None),
        P("dp", "tensor"),
        P("dp", "tensor"),
        P("dp", "tensor"),
        P("dp", None),
        P(),
    )
    return jax.shard_map(
        local, mesh=mesh, in_specs=placed, out_specs=P("dp", None, None), check_vma=False
    )
```

profile of v0, /device:TPU:0, one launch (start us, length us, event | category | flops | bytes accessed | tf_op | source)
XLA Modules:
  0.0 239.6 jit_solution(1877434285375292819)
XLA Ops:
  6.5 0.7 pad_add_fusion.1.s
  7.2 5.6 %shard_map.82 = (bf16[1024,640]{1,0:T(8,128)(2,1)}, bf16[1536,256]{1,0:T(8,128)(2,1)}, bf16[1024,640]{1,0:T(8,128)(2,1)}, bf16[1024,256]{1,0:T(8,128)(2,1)}, bf16[768,1024]{1,0:T(8,128)(2,1)}) custom-call(s32[3]{0:T(128)} %pad_add_fusion.1.s, bf16[1024,896]{1,0:T(8,128)(2,1)} %gate.1, bf16[1024,896]{1,0:T(8,128)(2,1)} %up.1, bf16[512,8192]{1,0:T(8,128)(2,1)} %refs_10_.3, ...), custom_call_target="tpu_custom_call" | custom-call | flops 1024 | bytes 1024 | tf_op jit(solution)/shard_map/pallas_call | solution.py:99
  12.9 2.1 collective-permute-start.2
  14.9 2.2 collective-permute-start.3
  17.2 3.0 %collective-permute-start.1 = (bf16[768,1024]{1,0:T(8,128)(2,1)}, bf16[768,1024]{1,0:T(8,128)(2,1)}, u32[]{:S(2)}, u32[]{:S(2)}) collective-permute-start(bf16[768,1024]{1,0:T(8,128)(2,1)} %get-tuple-element.62), channel_id=1, source_target_pairs={{0,18},{1,19},{4,22},{5,23},{8,26},{9,27},{12,30},{13,31},{16,2},{... | collective-permute-start | bytes 4718600 | tf_op jit(solution)/shard_map/ppermute | solution.py:58
  20.3 1.9 collective-permute-start.4
  22.3 2.8 %shard_map.83 = (bf16[768,512]{1,0:T(8,128)(2,1)}, bf16[784,512]{1,0:T(8,128)(2,1)}) custom-call(s32[1]{0:T(128)} %bitcast.ylo_ref, bf16[512,896]{1,0:T(8,128)(2,1)} %doc.4, bf16[256,896]{1,0:T(8,128)(2,1)} %query.3, s32[1,512]{1,0:T(1,128)} %ids.1), custom_call_target="tpu_custom_call" | custom-call | flops 1024 | bytes 1024 | tf_op jit(solution)/shard_map/pallas_call | solution.py:128
  25.6 0.6 gather_fusion
  26.2 0.7 concatenate.34.s
  26.8 0.7 concatenate.35.s
  27.6 0.6 concatenate.36.s
  28.3 33.3 %collective-permute-done.4 = bf16[1024,256]{1,0:T(8,128)(2,1)S(1)} collective-permute-done((bf16[1024,256]{1,0:T(8,128)(2,1)}, bf16[1024,256]{1,0:T(8,128)(2,1)S(1)}, u32[]{:S(2)}, u32[]{:S(2)}) %collective-permute-start.4) | collective-permute-done | bytes 524320 | tf_op jit(solution)/shard_map/ppermute | solution.py:58
  61.6 1.7 collective-permute-done.2.refs_1_.below
  63.3 2.3 collective-permute-done.3.refs_2_.above
  65.6 1.3 collective-permute-start.7
  67.0 2.0 collective-permute-start.8
  68.9 0.3 collective-permute-start.5
  69.3 3.4 %collective-permute-start.6 = (bf16[1024,640]{1,0:T(8,128)(2,1)}, bf16[1024,640]{1,0:T(8,128)(2,1)}, u32[]{:S(2)}, u32[]{:S(2)}) collective-permute-start(bf16[1024,640]{1,0:T(8,128)(2,1)} %collective-permute-done.refs_3_), channel_id=1, source_target_pairs={{0,96},{1,97},{4,100},{5,101},{8,104},{9,105},{12,108},{13,109},{1... | collective-permute-start | bytes 3932168 | tf_op jit(solution)/shard_map/ppermute | solution.py:58
  72.6 0.2 all-gather.4.cloned.1.call-done.refs_3_.refs_6_.refs_8_
  72.8 2.3 shard_map.85.mine
  75.1 1.6 collective-permute-start.9
  76.7 2.2 shard_map.87
  78.9 9.8 %shard_map.84.refs_16_ = f32[768,896]{1,0:T(8,128)} custom-call(s32[32]{0:T(128)} %concatenate.34.s, bf16[1024,640]{1,0:T(8,128)(2,1)} %get-tuple-element.63.refs_0_, bf16[1024,640]{1,0:T(8,128)(2,1)} %copy-done.6, bf16[1024,640]{1,0:T(8,128)(2,1)} %collective-permute-done.3.refs_2_.above, ...), custom_call_target="tpu_custom_call" | custom-call | flops 1024 | bytes 1024 | tf_op jit(solution)/shard_map/pallas_call | solution.py:335
  88.8 11.6 %collective-permute-done.9.theirs = bf16[64,8192]{1,0:T(8,128)(2,1)S(1)} collective-permute-done((bf16[64,8192]{1,0:T(8,128)(2,1)}, bf16[64,8192]{1,0:T(8,128)(2,1)S(1)}, u32[]{:S(2)}, u32[]{:S(2)}) %collective-permute-start.9) | collective-permute-done | bytes 1048608 | tf_op jit(solution)/shard_map/ppermute | solution.py:58
  100.4 1.0 copy-done.11
  101.4 8.6 %shard_map.86 = bf16[128,512]{1,0:T(8,128)(2,1)} custom-call(bf16[64,8192]{1,0:T(8,128)(2,1)} %shard_map.85.mine, bf16[64,8192]{1,0:T(8,128)(2,1)} %copy-done.11, bf16[512,8192]{1,0:T(8,128)(2,1)} %refs_10_.3), custom_call_target="tpu_custom_call" | custom-call | flops 1024 | bytes 1024 | tf_op jit(solution)/shard_map/pallas_call | solution.py:395
  110.0 1.9 collective-permute-done.5.below.refs_4_
  111.9 2.2 collective-permute-done.6.above.refs_5_
  114.2 0.5 collective-permute-start.11
  114.8 3.0 %shard_map.88 = (bf16[2,512,640]{2,1,0:T(8,128)(2,1)}, bf16[2,512,640]{2,1,0:T(8,128)(2,1)}, bf16[384,1024]{1,0:T(8,128)(2,1)}, bf16[384,1024]{1,0:T(8,128)(2,1)}) custom-call(bf16[1024,640]{1,0:T(8,128)(2,1)} %collective-permute-done.5.below.refs_4_, ...), custom_call_target="tpu_custom_call", output_to_operand_aliasing={{0}: (4, {}), {1}: (5, {})} | custom-call | flops 1024 | bytes 1024 | tf_op jit(solution)/shard_map/pallas_call | solution.py:162
  117.8 3.7 %collective-permute-start.16 = (bf16[1024,640]{1,0:T(8,128)(2,1)}, bf16[1024,640]{1,0:T(8,128)(2,1)}, u32[]{:S(2)}, u32[]{:S(2)}) collective-permute-start(bf16[1024,640]{1,0:T(8,128)(2,1)} %bitcast.44), channel_id=1, source_target_pairs={{0,96},{1,97},{4,100},{5,101},{8,104},{9,105},{12,108},{13,109},{1... | collective-permute-start | bytes 3932168 | tf_op jit(solution)/shard_map/ppermute | solution.py:58
  121.6 1.3 collective-permute-start.17
  122.9 0.3 collective-permute-start.13
  123.2 2.9 %collective-permute-start.14 = (bf16[384,1024]{1,0:T(8,128)(2,1)}, bf16[384,1024]{1,0:T(8,128)(2,1)}, u32[]{:S(2)}, u32[]{:S(2)}) collective-permute-start(bf16[384,1024]{1,0:T(8,128)(2,1)} %get-tuple-element.89), channel_id=1, source_target_pairs={{0,12},{1,13},{4,0},{5,1},{8,4},{9,5},{12,8},{13,9},{16,28},{17,29... | collective-permute-start | bytes 2359304 | tf_op jit(solution)/shard_map/ppermute | solution.py:58
  126.1 19.1 %shard_map.89 = (f32[768,896]{1,0:T(8,128)}, f32[768,896]{1,0:T(8,128)}) custom-call(s32[64]{0:T(128)} %concatenate.35.s, bf16[1024,640]{1,0:T(8,128)(2,1)} %get-tuple-element.63.refs_0_, bf16[1024,640]{1,0:T(8,128)(2,1)} %copy-done.6, bf16[1024,640]{1,0:T(8,128)(2,1)} %collective-permute-done.3.refs_2_.above, ...), custom_call_target="tpu_custom_call" | custom-call | flops 1024 | bytes 1024 | tf_op jit(solution)/shard_map/pallas_call | solution.py:335
  145.2 6.0 %collective-permute-done.15.refs_6_ = bf16[1024,640]{1,0:T(8,128)(2,1)} collective-permute-done((bf16[1024,640]{1,0:T(8,128)(2,1)}, bf16[1024,640]{1,0:T(8,128)(2,1)}, u32[]{:S(2)}, u32[]{:S(2)}) %collective-permute-start.15) | collective-permute-done | bytes 1310752 | tf_op jit(solution)/shard_map/ppermute | solution.py:58
  151.3 0.5 collective-permute-start.19
  151.8 2.0 collective-permute-done.18.refs_20_
  153.8 1.1 collective-permute-done.19.refs_21_
  154.9 0.9 copy-done.10
  155.8 10.1 %shard_map.90.refs_0_ = bf16[512,896]{1,0:T(8,128)(2,1)} custom-call(s32[64]{0:T(128)} %concatenate.36.s, bf16[1024,640]{1,0:T(8,128)(2,1)} %get-tuple-element.63.refs_0_, bf16[1024,640]{1,0:T(8,128)(2,1)} %copy-done.6, bf16[1024,640]{1,0:T(8,128)(2,1)} %collective-permute-done.3.refs_2_.above, bf16[1024,640]{1,0:T(8,128)(2,1)} %collective-permute-done.refs_3_, ...), custom_call_target="tpu_custom_call" | custom-call | flops 1024 | bytes 1024 | tf_op jit(solution)/shard_map/pallas_call | solution.py:335
  165.8 1.6 collective-permute-start.20
  167.4 1.7 collective-permute-start.21
  169.1 0.4 copy.13.refs_5_.refs_4_
  169.5 14.1 %shard_map.91.refs_3_.refs_2_ = bf16[1024,896]{1,0:T(8,128)(2,1)} custom-call(s32[64]{0:T(128)} %concatenate.36.s, bf16[1024,640]{1,0:T(8,128)(2,1)} %get-tuple-element.63.refs_0_, bf16[1024,640]{1,0:T(8,128)(2,1)} %copy-done.6, bf16[1024,640]{1,0:T(8,128)(2,1)} %collective-permute-done.3.refs_2_.above, bf16[1024,640]{1,0:T(8,128)(2,1)} %collective-permute-done.refs_3_, ...), custom_call_target="tpu_custom_call" | custom-call | flops 1024 | bytes 1024 | tf_op jit(solution)/shard_map/pallas_call | solution.py:335
  183.6 6.3 %collective-permute-done.20.refs_1_ = bf16[512,896]{1,0:T(8,128)(2,1)} collective-permute-done((bf16[512,896]{1,0:T(8,128)(2,1)}, bf16[512,896]{1,0:T(8,128)(2,1)}, u32[]{:S(2)}, u32[]{:S(2)}) %collective-permute-start.20) | collective-permute-done | bytes 917536 | tf_op jit(solution)/shard_map/ppermute | solution.py:58
  190.0 1.8 slice.16
  191.8 1.6 collective-permute-start.22
  193.4 1.8 slice.17
  195.2 1.7 collective-permute-start.23
  197.0 2.2 copy-done.2
  199.2 1.2 copy-done.5
  200.4 9.2 %shard_map.92.refs_6_ = f32[32,8]{1,0:T(8,128)S(1)} custom-call(s32[2]{0:T(128)S(1)} %pad_add_fusion.7.s, bf16[512,896]{1,0:T(8,128)(2,1)S(1)} %copy-done.5, bf16[512,896]{1,0:T(8,128)(2,1)} %collective-permute-done.20.refs_1_, bf16[512,896]{1,0:T(8,128)(2,1)} %collective-permute-done.21.refs_2_, bf16[1024,896]{1,0:T(8,128)(2,1)S(1)} %copy-done.4, ...), custom_call_target="tpu_custom_call" | custom-call | flops 1024 | bytes 1024 | tf_op jit(solution)/shard_map/pallas_call | solution.py:461
  209.6 4.0 %shard_map.93 = f32[32,8]{1,0:T(8,128)S(1)} custom-call(s32[2]{0:T(128)S(1)} %pad_add_fusion.7.s, bf16[256,896]{1,0:T(8,128)(2,1)S(1)} %collective-permute-done.22.refs_0_, bf16[256,896]{1,0:T(8,128)(2,1)} %collective-permute-done.23.refs_1_, bf16[1024,896]{1,0:T(8,128)(2,1)S(1)} %copy-done.4, bf16[4,4,2,2,4,16,512]{6,5,4,3,2,1,0:T(8,128)(2,1)S(1)} %bitcast.41, ...), custom_call_target="tpu_custom_call" | custom-call | flops 1024 | bytes 1024 | tf_op jit(solution)/shard_map/pallas_call | solution.py:461
  213.8 1.2 collective-permute-done.24
  214.9 0.6 collective-permute-start.25
  215.5 3.2 %collective-permute-done.25 = f32[32,8]{1,0:T(8,128)S(1)} collective-permute-done((f32[32,8]{1,0:T(8,128)S(1)}, f32[32,8]{1,0:T(8,128)S(1)}, u32[]{:S(2)}, u32[]{:S(2)}) %collective-permute-start.25) | collective-permute-done | bytes 1056 | tf_op jit(solution)/shard_map/ppermute | solution.py:58
  218.7 2.0 collective-permute-start.26
  220.6 3.0 %collective-permute-done.26 = f32[32,8]{1,0:T(8,128)S(1)} collective-permute-done((f32[32,8]{1,0:T(8,128)S(1)}, f32[32,8]{1,0:T(8,128)S(1)}, u32[]{:S(2)}, u32[]{:S(2)}) %collective-permute-start.26) | collective-permute-done | bytes 1056 | tf_op jit(solution)/shard_map/ppermute | solution.py:58
  223.6 1.5 collective-permute-start.27
  225.2 2.2 collective-permute-done.27
  227.4 3.1 %collective-permute-start.28 = (f32[32,8]{1,0:T(8,128)S(1)}, f32[32,8]{1,0:T(8,128)S(1)}, u32[]{:S(2)}, u32[]{:S(2)}) collective-permute-start(f32[32,8]{1,0:T(8,128)S(1)} %add.393), channel_id=1, source_target_pairs={{0,18},{1,19},{4,22},{5,23},{8,26},{9,27},{12,30},{13,31},{16,2},{... | collective-permute-start | bytes 3080 | tf_op jit(solution)/shard_map/ppermute | solution.py:58
  230.4 1.9 collective-permute-done.28
  232.4 0.7 copy.14
  (80 shorter events, 1.7 us)
Async XLA Ops:
  6.5 19.0 %copy-start = (s32[8,256]{1,0:T(8,128)S(1)}, s32[8,256]{1,0:T(8,128)}, u32[]{:S(2)}) copy-start(s32[8,256]{1,0:T(8,128)} %param.15) | copy-start | bytes 24580
  6.5 66.3 %all-gather.4.cloned.1.call-start = ((), (), s32[]{:S(2)}) async-start(), calls=%async_computation | async-start | bytes 3932160 | tf_op jit(solution)/shard_map/all_gather | solution.py:516
  12.8 113.3 %all-gather.6.cloned.1.call-start = ((), (), s32[]{:S(2)}) async-start(), calls=%async_computation.1 | async-start | bytes 2621440 | tf_op jit(solution)/shard_map/all_gather | solution.py:527
  12.9 50.4 %collective-permute-start.2 = (bf16[1024,640]{1,0:T(8,128)(2,1)}, bf16[1024,640]{1,0:T(8,128)(2,1)S(1)}, u32[]{:S(2)}, u32[]{:S(2)}) collective-permute-start(bf16[1024,640]{1,0:T(8,128)(2,1)} %get-tuple-element.63.refs_0_), channel_id=1, source_target_pairs={{0,32},{1,33},{4,36},{5,37},{8,40},{9,41},{12,44},{13,45},{16,48},... | collective-permute-start | bytes 3932168 | tf_op jit(solution)/shard_map/ppermute | solution.py:58
  14.9 50.6 %collective-permute-start.3 = (bf16[1024,640]{1,0:T(8,128)(2,1)}, bf16[1024,640]{1,0:T(8,128)(2,1)}, u32[]{:S(2)}, u32[]{:S(2)}) collective-permute-start(bf16[1024,640]{1,0:T(8,128)(2,1)} %get-tuple-element.63.refs_0_), channel_id=1, source_target_pairs={{0,96},{1,97},{4,100},{5,101},{8,104},{9,105},{12,108},{13,109},{1... | collective-permute-start | bytes 3932168 | tf_op jit(solution)/shard_map/ppermute | solution.py:58
  17.2 48.4 %collective-permute-start.1 = (bf16[768,1024]{1,0:T(8,128)(2,1)}, bf16[768,1024]{1,0:T(8,128)(2,1)}, u32[]{:S(2)}, u32[]{:S(2)}) collective-permute-start(bf16[768,1024]{1,0:T(8,128)(2,1)} %get-tuple-element.62), channel_id=1, source_target_pairs={{0,18},{1,19},{4,22},{5,23},{8,26},{9,27},{12,30},{13,31},{16,2},{... | collective-permute-start | bytes 4718600 | tf_op jit(solution)/shard_map/ppermute | solution.py:58
  20.2 41.4 %collective-permute-start = (bf16[1024,640]{1,0:T(8,128)(2,1)}, bf16[1024,640]{1,0:T(8,128)(2,1)}, u32[]{:S(2)}, u32[]{:S(2)}) collective-permute-start(bf16[1024,640]{1,0:T(8,128)(2,1)} %get-tuple-element.61), channel_id=1, source_target_pairs={{0,16},{1,17},{4,20},{5,21},{8,24},{9,25},{12,28},{13,29},{16,0},{... | collective-permute-start | bytes 3932168 | tf_op jit(solution)/shard_map/ppermute | solution.py:58
  20.3 41.3 %collective-permute-start.4 = (bf16[1024,256]{1,0:T(8,128)(2,1)}, bf16[1024,256]{1,0:T(8,128)(2,1)S(1)}, u32[]{:S(2)}, u32[]{:S(2)}) collective-permute-start(bf16[1024,256]{1,0:T(8,128)(2,1)} %get-tuple-element.64), channel_id=1, source_target_pairs={{0,16},{1,17},{4,20},{5,21},{8,24},{9,25},{12,28},{13,29},{16,0},{... | collective-permute-start | bytes 1572872 | tf_op jit(solution)/shard_map/ppermute | solution.py:58
  61.6 4.0 %copy-start.12 = (bf16[1024,256]{1,0:T(8,128)(2,1)}, bf16[1024,256]{1,0:T(8,128)(2,1)S(1)}, u32[]{:S(2)}) copy-start(bf16[1024,256]{1,0:T(8,128)(2,1)S(1)} %collective-permute-done.4) | copy-start | bytes 1572868
  63.2 11.8 %copy-start.6 = (bf16[1024,640]{1,0:T(8,128)(2,1)}, bf16[1024,640]{1,0:T(8,128)(2,1)S(1)}, u32[]{:S(2)}) copy-start(bf16[1024,640]{1,0:T(8,128)(2,1)S(1)} %collective-permute-done.2.refs_1_.below) | copy-start | bytes 3932164
  65.6 131.4 %all-gather.8.cloned.1.call-start = ((), (), s32[]{:S(2)}) async-start(), calls=%async_computation.2 | async-start | bytes 4325376 | tf_op jit(solution)/shard_map/all_gather | solution.py:553
  65.6 48.5 %collective-permute-start.7 = (bf16[768,1024]{1,0:T(8,128)(2,1)}, bf16[768,1024]{1,0:T(8,128)(2,1)}, u32[]{:S(2)}, u32[]{:S(2)}) collective-permute-start(bf16[768,1024]{1,0:T(8,128)(2,1)} %collective-permute-done.1.refs_10_.refs_12_), channel_id=1, source_target_pairs={{0,4},{1,5},{4,8},{5,9},{8,12},{9,13},{12,0},{13,1},{16,20},{17,21... | collective-permute-start | bytes 4718600 | tf_op jit(solution)/shard_map/ppermute | solution.py:58
  67.0 47.2 %collective-permute-start.8 = (bf16[768,1024]{1,0:T(8,128)(2,1)}, bf16[768,1024]{1,0:T(8,128)(2,1)}, u32[]{:S(2)}, u32[]{:S(2)}) collective-permute-start(bf16[768,1024]{1,0:T(8,128)(2,1)} %collective-permute-done.1.refs_10_.refs_12_), channel_id=1, source_target_pairs={{0,12},{1,13},{4,0},{5,1},{8,4},{9,5},{12,8},{13,9},{16,28},{17,29... | collective-permute-start | bytes 4718600 | tf_op jit(solution)/shard_map/ppermute | solution.py:58
  68.9 43.0 %collective-permute-start.5 = (bf16[1024,640]{1,0:T(8,128)(2,1)}, bf16[1024,640]{1,0:T(8,128)(2,1)}, u32[]{:S(2)}, u32[]{:S(2)}) collective-permute-start(bf16[1024,640]{1,0:T(8,128)(2,1)} %collective-permute-done.refs_3_), channel_id=1, source_target_pairs={{0,32},{1,33},{4,36},{5,37},{8,40},{9,41},{12,44},{13,45},{16,48},... | collective-permute-start | bytes 3932168 | tf_op jit(solution)/shard_map/ppermute | solution.py:58
  69.3 44.8 %collective-permute-start.6 = (bf16[1024,640]{1,0:T(8,128)(2,1)}, bf16[1024,640]{1,0:T(8,128)(2,1)}, u32[]{:S(2)}, u32[]{:S(2)}) collective-permute-start(bf16[1024,640]{1,0:T(8,128)(2,1)} %collective-permute-done.refs_3_), channel_id=1, source_target_pairs={{0,96},{1,97},{4,100},{5,101},{8,104},{9,105},{12,108},{13,109},{1... | collective-permute-start | bytes 3932168 | tf_op jit(solution)/shard_map/ppermute | solution.py:58
  75.1 25.3 %collective-permute-start.9 = (bf16[64,8192]{1,0:T(8,128)(2,1)}, bf16[64,8192]{1,0:T(8,128)(2,1)S(1)}, u32[]{:S(2)}, u32[]{:S(2)}) collective-permute-start(bf16[64,8192]{1,0:T(8,128)(2,1)} %shard_map.85.mine), channel_id=1, source_target_pairs={{0,16},{1,17},{4,20},{5,21},{8,24},{9,25},{12,28},{13,29},{16,0},{... | collective-permute-start | bytes 3145736 | tf_op jit(solution)/shard_map/ppermute | solution.py:58
  100.4 1.0 copy-start.11
  114.2 7.4 %collective-permute-start.10 = (bf16[768,1024]{1,0:T(8,128)(2,1)}, bf16[768,1024]{1,0:T(8,128)(2,1)S(1)}, u32[]{:S(2)}, u32[]{:S(2)}) collective-permute-start(bf16[768,1024]{1,0:T(8,128)(2,1)} %collective-permute-done.1.refs_10_.refs_12_), channel_id=1, source_target_pairs={{0,1},{1,0},{4,5},{5,4},{8,9},{9,8},{12,13},{13,12},{16,17},{17,16... | collective-permute-start | bytes 4718600 | tf_op jit(solution)/shard_map/ppermute | solution.py:58
  114.2 8.6 %collective-permute-start.11 = (bf16[768,1024]{1,0:T(8,128)(2,1)}, bf16[768,1024]{1,0:T(8,128)(2,1)}, u32[]{:S(2)}, u32[]{:S(2)}) collective-permute-start(bf16[768,1024]{1,0:T(8,128)(2,1)} %collective-permute-done.7.x_below.refs_12_.refs_14_), channel_id=1, source_target_pairs={{0,1},{1,0},{4,5},{5,4},{8,9},{9,8},{12,13},{13,12},{16,17},{17,16... | collective-permute-start | bytes 4718600 | tf_op jit(solution)/shard_map/ppermute | solution.py:58
  114.7 8.1 %collective-permute-start.12 = (bf16[768,1024]{1,0:T(8,128)(2,1)}, bf16[768,1024]{1,0:T(8,128)(2,1)}, u32[]{:S(2)}, u32[]{:S(2)}) collective-permute-start(bf16[768,1024]{1,0:T(8,128)(2,1)} %collective-permute-done.8.x_above.refs_14_.refs_16_), channel_id=1, source_target_pairs={{0,1},{1,0},{4,5},{5,4},{8,9},{9,8},{12,13},{13,12},{16,17},{17,16... | collective-permute-start | bytes 4718600 | tf_op jit(solution)/shard_map/ppermute | solution.py:58
  117.8 33.4 %collective-permute-start.15 = (bf16[1024,640]{1,0:T(8,128)(2,1)}, bf16[1024,640]{1,0:T(8,128)(2,1)}, u32[]{:S(2)}, u32[]{:S(2)}) collective-permute-start(bf16[1024,640]{1,0:T(8,128)(2,1)} %bitcast.43), channel_id=1, source_target_pairs={{0,32},{1,33},{4,36},{5,37},{8,40},{9,41},{12,44},{13,45},{16,48},... | collective-permute-start | bytes 3932168 | tf_op jit(solution)/shard_map/ppermute | solution.py:58
  117.8 33.3 %collective-permute-start.16 = (bf16[1024,640]{1,0:T(8,128)(2,1)}, bf16[1024,640]{1,0:T(8,128)(2,1)}, u32[]{:S(2)}, u32[]{:S(2)}) collective-permute-start(bf16[1024,640]{1,0:T(8,128)(2,1)} %bitcast.44), channel_id=1, source_target_pairs={{0,96},{1,97},{4,100},{5,101},{8,104},{9,105},{12,108},{13,109},{1... | collective-permute-start | bytes 3932168 | tf_op jit(solution)/shard_map/ppermute | solution.py:58
  121.6 4.5 %copy-start.7 = (bf16[768,1024]{1,0:T(8,128)(2,1)}, bf16[768,1024]{1,0:T(8,128)(2,1)S(1)}, u32[]{:S(2)}) copy-start(bf16[768,1024]{1,0:T(8,128)(2,1)S(1)} %collective-permute-done.10.refs_11_.refs_13_) | copy-start | bytes 4718596
  121.6 23.6 %collective-permute-start.17 = (bf16[784,512]{1,0:T(8,128)(2,1)}, bf16[784,512]{1,0:T(8,128)(2,1)S(1)}, u32[]{:S(2)}, u32[]{:S(2)}) collective-permute-start(bf16[784,512]{1,0:T(8,128)(2,1)} %get-tuple-element.100), channel_id=1, source_target_pairs={{0,16},{1,17},{4,20},{5,21},{8,24},{9,25},{12,28},{13,29},{16,0},{... | collective-permute-start | bytes 2408456 | tf_op jit(solution)/shard_map/ppermute | solution.py:58
  122.9 28.3 %collective-permute-start.13 = (bf16[384,1024]{1,0:T(8,128)(2,1)}, bf16[384,1024]{1,0:T(8,128)(2,1)}, u32[]{:S(2)}, u32[]{:S(2)}) collective-permute-start(bf16[384,1024]{1,0:T(8,128)(2,1)} %get-tuple-element.88), channel_id=1, source_target_pairs={{0,4},{1,5},{4,8},{5,9},{8,12},{9,13},{12,0},{13,1},{16,20},{17,21... | collective-permute-start | bytes 2359304 | tf_op jit(solution)/shard_map/ppermute | solution.py:58
  123.2 28.0 %collective-permute-start.14 = (bf16[384,1024]{1,0:T(8,128)(2,1)}, bf16[384,1024]{1,0:T(8,128)(2,1)}, u32[]{:S(2)}, u32[]{:S(2)}) collective-permute-start(bf16[384,1024]{1,0:T(8,128)(2,1)} %get-tuple-element.89), channel_id=1, source_target_pairs={{0,12},{1,13},{4,0},{5,1},{8,4},{9,5},{12,8},{13,9},{16,28},{17,29... | collective-permute-start | bytes 2359304 | tf_op jit(solution)/shard_map/ppermute | solution.py:58
  145.2 9.7 %copy-start.8 = (bf16[784,512]{1,0:T(8,128)(2,1)}, bf16[784,512]{1,0:T(8,128)(2,1)S(1)}, u32[]{:S(2)}) copy-start(bf16[784,512]{1,0:T(8,128)(2,1)S(1)} %collective-permute-done.17.refs_25_) | copy-start | bytes 2408452
  151.2 2.6 %collective-permute-start.18 = (bf16[384,1024]{1,0:T(8,128)(2,1)}, bf16[384,1024]{1,0:T(8,128)(2,1)S(1)}, u32[]{:S(2)}, u32[]{:S(2)}) collective-permute-start(bf16[384,1024]{1,0:T(8,128)(2,1)} %collective-permute-done.13.refs_18_), channel_id=1, source_target_pairs={{0,1},{1,0},{4,5},{5,4},{8,9},{9,8},{12,13},{13,12},{16,17},{17,16... | collective-permute-start | bytes 2359304 | tf_op jit(solution)/shard_map/ppermute | solution.py:58
  151.3 3.6 %collective-permute-start.19 = (bf16[384,1024]{1,0:T(8,128)(2,1)}, bf16[384,1024]{1,0:T(8,128)(2,1)S(1)}, u32[]{:S(2)}, u32[]{:S(2)}) collective-permute-start(bf16[384,1024]{1,0:T(8,128)(2,1)} %collective-permute-done.14.refs_19_), channel_id=1, source_target_pairs={{0,1},{1,0},{4,5},{5,4},{8,9},{9,8},{12,13},{13,12},{16,17},{17,16... | collective-permute-start | bytes 2359304 | tf_op jit(solution)/shard_map/ppermute | solution.py:58
  153.8 1.1 copy-start.9
  154.9 0.9 copy-start.10
  165.8 24.1 %collective-permute-start.20 = (bf16[512,896]{1,0:T(8,128)(2,1)}, bf16[512,896]{1,0:T(8,128)(2,1)}, u32[]{:S(2)}, u32[]{:S(2)}) collective-permute-start(bf16[512,896]{1,0:T(8,128)(2,1)} %shard_map.90.refs_0_), channel_id=1, source_target_pairs={{0,32},{1,33},{4,36},{5,37},{8,40},{9,41},{12,44},{13,45},{16,48},... | collective-permute-start | bytes 2752520 | tf_op jit(solution)/shard_map/ppermute | solution.py:58
  167.4 22.6 %collective-permute-start.21 = (bf16[512,896]{1,0:T(8,128)(2,1)}, bf16[512,896]{1,0:T(8,128)(2,1)}, u32[]{:S(2)}, u32[]{:S(2)}) collective-permute-start(bf16[512,896]{1,0:T(8,128)(2,1)} %shard_map.90.refs_0_), channel_id=1, source_target_pairs={{0,96},{1,97},{4,100},{5,101},{8,104},{9,105},{12,108},{13,109},{1... | collective-permute-start | bytes 2752520 | tf_op jit(solution)/shard_map/ppermute | solution.py:58
  169.5 27.4 %copy-start.13 = (s32[1,512]{1,0:T(1,128)S(1)}, s32[1,512]{1,0:T(1,128)}, u32[]{:S(2)}) copy-start(s32[1,512]{1,0:T(1,128)} %ids.1) | copy-start | bytes 6148
  183.6 13.4 %copy-start.4 = (bf16[1024,896]{1,0:T(8,128)(2,1)S(1)}, bf16[1024,896]{1,0:T(8,128)(2,1)}, u32[]{:S(2)}) copy-start(bf16[1024,896]{1,0:T(8,128)(2,1)} %shard_map.91.refs_3_.refs_2_) | copy-start | bytes 5505028
  191.8 17.8 %collective-permute-start.22 = (bf16[256,896]{1,0:T(8,128)(2,1)}, bf16[256,896]{1,0:T(8,128)(2,1)S(1)}, u32[]{:S(2)}, u32[]{:S(2)}) collective-permute-start(bf16[256,896]{1,0:T(8,128)(2,1)} %slice.16), channel_id=1, source_target_pairs={{0,32},{1,33},{4,36},{5,37},{8,40},{9,41},{12,44},{13,45},{16,48},... | collective-permute-start | bytes 1376264 | tf_op jit(solution)/shard_map/ppermute | solution.py:58
  195.2 14.4 %collective-permute-start.23 = (bf16[256,896]{1,0:T(8,128)(2,1)}, bf16[256,896]{1,0:T(8,128)(2,1)}, u32[]{:S(2)}, u32[]{:S(2)}) collective-permute-start(bf16[256,896]{1,0:T(8,128)(2,1)} %slice.17), channel_id=1, source_target_pairs={{0,96},{1,97},{4,100},{5,101},{8,104},{9,105},{12,108},{13,109},{1... | collective-permute-start | bytes 1376264 | tf_op jit(solution)/shard_map/ppermute | solution.py:58
  197.0 2.2 copy-start.2
  199.2 1.2 copy-start.5
  200.4 9.3 %copy-start.3 = (bf16[4096,512]{1,0:T(8,128)(2,1)S(1)}, bf16[4096,512]{1,0:T(8,128)(2,1)}, u32[]{:S(2)}) copy-start(bf16[4096,512]{1,0:T(8,128)(2,1)} %all-gather.8.cloned.1.call-done) | copy-start | bytes 12582916
  209.6 23.5 %copy-start.1 = (s32[8,256]{1,0:T(8,128)S(1)}, s32[8,256]{1,0:T(8,128)}, u32[]{:S(2)}) copy-start(s32[8,256]{1,0:T(8,128)} %param.15) | copy-start | bytes 24580
  213.7 1.3 collective-permute-start.24
  214.9 3.7 %collective-permute-start.25 = (f32[32,8]{1,0:T(8,128)S(1)}, f32[32,8]{1,0:T(8,128)S(1)}, u32[]{:S(2)}, u32[]{:S(2)}) collective-permute-start(f32[32,8]{1,0:T(8,128)S(1)} %add.390), channel_id=1, source_target_pairs={{0,4},{1,5},{4,0},{5,1},{8,12},{9,13},{12,8},{13,9},{16,20},{17,21... | collective-permute-start | bytes 3080 | tf_op jit(solution)/shard_map/ppermute | solution.py:58
  218.7 4.9 %collective-permute-start.26 = (f32[32,8]{1,0:T(8,128)S(1)}, f32[32,8]{1,0:T(8,128)S(1)}, u32[]{:S(2)}, u32[]{:S(2)}) collective-permute-start(f32[32,8]{1,0:T(8,128)S(1)} %add.391), channel_id=1, source_target_pairs={{0,12},{1,13},{4,8},{5,9},{8,4},{9,5},{12,0},{13,1},{16,28},{17,29... | collective-permute-start | bytes 3080 | tf_op jit(solution)/shard_map/ppermute | solution.py:58
  223.6 3.7 %collective-permute-start.27 = (f32[32,8]{1,0:T(8,128)S(1)}, f32[32,8]{1,0:T(8,128)S(1)}, u32[]{:S(2)}, u32[]{:S(2)}) collective-permute-start(f32[32,8]{1,0:T(8,128)S(1)} %add.392), channel_id=1, source_target_pairs={{0,16},{1,17},{4,20},{5,21},{8,24},{9,25},{12,28},{13,29},{16,0},{... | collective-permute-start | bytes 3080 | tf_op jit(solution)/shard_map/ppermute | solution.py:58
  227.4 4.9 %collective-permute-start.28 = (f32[32,8]{1,0:T(8,128)S(1)}, f32[32,8]{1,0:T(8,128)S(1)}, u32[]{:S(2)}, u32[]{:S(2)}) collective-permute-start(f32[32,8]{1,0:T(8,128)S(1)} %add.393), channel_id=1, source_target_pairs={{0,18},{1,19},{4,22},{5,23},{8,26},{9,27},{12,30},{13,31},{16,2},{... | collective-permute-start | bytes 3080 | tf_op jit(solution)/shard_map/ppermute | solution.py:58
Sparse Core Ops, SparseCore 0:
  12.9 59.8 all-gather.3
  74.5 42.1 all-gather.5
  118.9 48.3 all-gather.7
where the time goes:
time: 240 us
  Pallas kernels  90.7 us (38%)
  waiting for transfers between devices  80.2 us (33%)
  starting transfers between devices  41.2 us (17%)
  between operations  13.4 us (6%)
  local copies, waits for them, and re-layouts  12.6 us (5%)
    ppermute x29, waiting for transfers between devices, send(): return lax.ppermute(v, AX, p)  80 us
    pallas_call x4, Pallas kernels, factors(): pl.pallas_call(functools.partial(factor_kernel, phases, m, row, len(ws),...  53 us
    ppermute x29, starting transfers between devices, send(): return lax.ppermute(v, AX, p)  41.2 us
    pallas_call x2, Pallas kernels, score_sums(): pl.pallas_call(functools.partial(score_kernel, first, len(queries)), grid...  13.3 us
    pallas_call x1, Pallas kernels, gram_part(): pl.pallas_call(gram_kernel, grid=(8,), in_specs=[few, few, pl.BlockSpec((...  8.56 us
    pallas_call x1, Pallas kernels, pack(): pl.pallas_call(pack_kernel, grid_spec=pltpu.PrefetchScalarGridSpec(num_sc...  5.6 us
    unnamed x29, local copies, waits for them, and re-layouts  5.3 us
    pallas_call x2, Pallas kernels, halves(): pl.pallas_call(halves_b_kernel if into else halves_a_kernel, grid=(steps,...  5.21 us
  transfers between devices with their start and end apart: 32, of which 17 were waited for; matrix products, arithmetic and copies ran while one was open for 3% of the time, Pallas kernels for 34%

commit v1 on v0

--- a/solution.py
+++ b/solution.py
@@ -178,7 +178,7 @@
     return gate_factor, up_factor
 
 
-def factor_kernel(phases, m, row, nw, nt, nx, s, *refs):
+def factor_kernel(phases, m, row, split, nw, nt, nx, s, *refs):
     def take(n):
         nonlocal refs
         got, refs = refs[:n], refs[n:]
@@ -188,7 +188,7 @@
     ws, thins, own_x, other_x = take(nw), take(nt), take(2), take(nx)
     befores = [None if begins else take(1)[0] for _, _, begins, _ in phases]
     hidden = [take(1)[0] for _ in phases] if ends else None
-    outs = take(1 if ends else len(phases))
+    outs = take(1 if ends and not split else len(phases))
     acc, wv, xv, wsem, xsem, bsem, osem = refs[:7]
     hv, hsem = refs[7:] if ends else (None, None)
     steps = [(p, k) for p, phase in enumerate(phases) for k in range(phase[1])]
@@ -249,7 +249,7 @@
 
     def finish(p):
         hidden_copy(p).wait()
-        dst, to = outs[0], slice(p * m, p * m + m)
+        dst, to = (outs[p], slice(0, m)) if split else (outs[0], slice(p * m, p * m + m))
         g, u = gated(hv[p, :, :256].astype(F32), acc[p, :, :256], acc[p, :, 256:512])
         dst[to, :256] = g
         dst[to, 256:512] = u
@@ -319,7 +319,7 @@
                 out_copy(p).wait()
 
 
-def factors(phases, scalars, ws, thins, own, other=(), befores=(), hidden=(), rows=(0, ROWS)):
+def factors(phases, scalars, ws, thins, own, other=(), befores=(), hidden=(), rows=(0, ROWS), split=False):
     row, m = rows
     ends = phases[0][3]
     hbm = pl.BlockSpec(memory_space=pl.ANY)
@@ -327,13 +327,14 @@
     args = [*ws, *thins, *own, *other, *befores, *hidden]
     in_specs = [hbm] * len(args)
     if ends:
-        out_shape = [jax.ShapeDtypeStruct((len(phases) * m, 896), BF16)]
-        out_specs = [whole(out_shape[0])]
+        count = len(phases) if split else 1
+        out_shape = [jax.ShapeDtypeStruct((len(phases) // count * m, 896), BF16)] * count
+        out_specs = [whole(v) for v in out_shape]
     else:
         out_shape = [jax.ShapeDtypeStruct((m, 896), F32)] * len(phases)
         out_specs = [hbm] * len(phases)
     return pl.pallas_call(
-        functools.partial(factor_kernel, phases, m, row, len(ws), len(thins), len(other)),
+        functools.partial(factor_kernel, phases, m, row, split, len(ws), len(thins), len(other)),
         grid_spec=pltpu.PrefetchScalarGridSpec(
             num_scalar_prefetch=1,
             grid=(sum(phase[1] for phase in phases),),
@@ -409,7 +410,7 @@
 
 
 def score_kernel(first, count, s, *refs):
-    qs, (d, gram, ids, docs, before, out, f, b, acc) = refs[:count], refs[count:]
+    qs, (d, gram, ids, docs, before, out, f, b, acc) = refs[: 2 * count], refs[2 * count :]
     i = pl.program_id(0)
     r = first + i
     z, ylo = s[0], s[1]
@@ -418,15 +419,12 @@
     def _():
         acc[...] = jnp.zeros_like(acc)
 
-    if first == 3:
-        f[:QTOK] = qs[0][...]
-        f[QTOK:] = qs[1][...]
-    else:
-        for n in range(count):
-
-            @pl.when(i == n)
-            def _():
-                f[...] = qs[n][...]
+    for n in range(count):
+
+        @pl.when(i == n)
+        def _():
+            f[:QTOK] = qs[2 * n][...]
+            f[QTOK:] = qs[2 * n + 1][...]
 
     for flip in (0, 1):
         b[...] = lax.dot_general(f[flip * QTOK : flip * QTOK + QTOK], d[...], NT, preferred_element_type=F32)
@@ -459,10 +457,10 @@
     whole = lambda v: pl.BlockSpec(v.shape, lambda r, s: (0, 0))
     planes = pl.BlockSpec((4, 4, 2, 2, 1, 16, TOK), lambda r, s: (0, 0, 0, 0, lax.rem(s[0] + hop(first + r), 4), 0, 0))
     return pl.pallas_call(
-        functools.partial(score_kernel, first, len(queries)),
+        functools.partial(score_kernel, first, len(queries) // 2),
         grid_spec=pltpu.PrefetchScalarGridSpec(
             num_scalar_prefetch=1,
-            grid=(1 if first == 3 else len(queries),),
+            grid=(len(queries) // 2,),
             in_specs=[whole(v) for v in (*queries, documents)]
             + [planes, pl.BlockSpec((2 * QTOK, 1), lambda r, s: (first + r, 0)), whole(docs), whole(before)],
             out_specs=whole(before),
@@ -559,19 +557,19 @@
 
     rest = (("own", 2, False, True), ("other", 4, False, True))
     parts, grads = (own_part, other_part), (mine, theirs)
-    (q,) = factors(rest, late, all_w, thins, own, all_x, parts, grads, (TOK, QTOK))
-    q, own_part, ids_too = tie(q, own_part, theirs[ROWS : ROWS + 1])
+    q = factors(rest, late, all_w, thins, own, all_x, parts, grads, (TOK, QTOK), True)
+    *q, own_part, ids_too = tie(*q, own_part, theirs[ROWS : ROWS + 1])
     ids_too = ids_too.astype(jnp.int32)
     lower, upper = jnp.where(ylo == 0, doc_ids, ids_too), jnp.where(ylo == 0, ids_too, doc_ids)
     both = jnp.concatenate([lower, upper + DOCS], 1)
     docs = (both == jnp.arange(2 * DOCS, dtype=jnp.int32)[:, None]).astype(F32)
-    q_below, q_above = send(q, ZP), send(q, ZM)
+    q_below, q_above = [send(v, ZP) for v in q], [send(v, ZM) for v in q]
     (d,) = factors(rest, late, all_w, thins, own, all_x, (own_part, other_part), grads, (0, TOK))
-    q_below, q_above, d = tie(q_below, q_above, d)
-    q_far0, q_far1 = send(q_below[:QTOK], ZP), send(q_above[QTOK:], ZM)
+    *around, d = tie(*q_below, *q_above, d)
+    q_far0, q_far1 = send(around[0], ZP), send(around[3], ZM)
 
     scores = jnp.zeros((8 * QS, 2 * DOCS), F32)
-    scores = score_sums(0, where, (q, q_below, q_above), d, gram, ids, docs, scores)
+    scores = score_sums(0, where, (*q, *around), d, gram, ids, docs, scores)
     scores = score_sums(3, where, (q_far0, q_far1), d, gram, ids, docs, scores)
 
     for p in (CORE, X1, X3, PARTNER, OTHER):

time: 240 us -> 238 us (level)
  local copies, waits for them, and re-layouts: 12.6 us -> 9.12 us
    slice x3 -> x1, local copies, waits for them, and re-layouts: 3.67 us -> 0.01 us  [local(): *q, own_part, ids_too = tie(*q, own_part, theirs[ROWS:ROWS + 1])]
    ppermute x29 -> x31, waiting for transfers between devices: 80 us -> 81.1 us  [send(): return lax.ppermute(v, AX, p)]
    unnamed x29 -> x37, local copies, waits for them, and re-layouts: 5.3 us -> 5.63 us
    ppermute x29 -> x31, starting transfers between devices: 41.2 us -> 41.5 us  [send(): return lax.ppermute(v, AX, p)]
  transfers between devices with their start and end apart: 32 -> 34, of which waited for: 17 -> 17; matrix products, arithmetic and copies ran while one was open for 3% -> 1% of each run, Pallas kernels for 34% -> 34%
where the time goes in v1:
time: 238 us
  Pallas kernels  90.6 us (38%)
  waiting for transfers between devices  81.5 us (34%)
  starting transfers between devices  41.5 us (17%)
  between operations  13.5 us (6%)
  local copies, waits for them, and re-layouts  9.12 us (4%)
    ppermute x31, waiting for transfers between devices, send(): return lax.ppermute(v, AX, p)  81.1 us
    pallas_call x4, Pallas kernels, factors(): pl.pallas_call(functools.partial(factor_kernel, phases, m, row, split, le...  53.2 us
    ppermute x31, starting transfers between devices, send(): return lax.ppermute(v, AX, p)  41.5 us
    pallas_call x2, Pallas kernels, score_sums(): pl.pallas_call(functools.partial(score_kernel, first, len(queries) // 2),...  13 us
    pallas_call x1, Pallas kernels, gram_part(): pl.pallas_call(gram_kernel, grid=(8,), in_specs=[few, few, pl.BlockSpec((...  8.61 us
    unnamed x37, local copies, waits for them, and re-layouts  5.63 us
    pallas_call x1, Pallas kernels, pack(): pl.pallas_call(pack_kernel, grid_spec=pltpu.PrefetchScalarGridSpec(num_sc...  5.57 us
    pallas_call x2, Pallas kernels, halves(): pl.pallas_call(halves_b_kernel if into else halves_a_kernel, grid=(steps,...  5.26 us
  transfers between devices with their start and end apart: 34, of which 17 were waited for; matrix products, arithmetic and copies ran while one was open for 1% of the time, Pallas kernels for 34%

profile of v1, /device:TPU:0, one launch (start us, length us, event | category | flops | bytes accessed | tf_op | source)
XLA Modules:
  0.0 237.6 jit_solution(14196338305230466512)
XLA Ops:
  6.5 0.6 pad_add_fusion.1.s
  7.1 5.6 %shard_map.82 = (bf16[1024,640]{1,0:T(8,128)(2,1)}, bf16[1536,256]{1,0:T(8,128)(2,1)}, bf16[1024,640]{1,0:T(8,128)(2,1)}, bf16[1024,256]{1,0:T(8,128)(2,1)}, bf16[768,1024]{1,0:T(8,128)(2,1)}) custom-call(s32[3]{0:T(128)} %pad_add_fusion.1.s, bf16[1024,896]{1,0:T(8,128)(2,1)} %gate.1, bf16[1024,896]{1,0:T(8,128)(2,1)} %up.1, bf16[512,8192]{1,0:T(8,128)(2,1)} %refs_10_.3, ...), custom_call_target="tpu_custom_call" | custom-call | flops 1024 | bytes 1024 | tf_op jit(solution)/shard_map/pallas_call | solution.py:99
  12.8 2.1 collective-permute-start.2
  14.9 2.2 collective-permute-start.3
  17.1 3.0 %collective-permute-start.1 = (bf16[768,1024]{1,0:T(8,128)(2,1)}, bf16[768,1024]{1,0:T(8,128)(2,1)}, u32[]{:S(2)}, u32[]{:S(2)}) collective-permute-start(bf16[768,1024]{1,0:T(8,128)(2,1)} %get-tuple-element.67), channel_id=1, source_target_pairs={{0,18},{1,19},{4,22},{5,23},{8,26},{9,27},{12,30},{13,31},{16,2},{... | collective-permute-start | bytes 4718600 | tf_op jit(solution)/shard_map/ppermute | solution.py:58
  20.1 0.1 collective-permute-start
  20.2 1.9 collective-permute-start.4
  22.2 2.8 %shard_map.83 = (bf16[768,512]{1,0:T(8,128)(2,1)}, bf16[784,512]{1,0:T(8,128)(2,1)}) custom-call(s32[1]{0:T(128)} %bitcast.ylo_ref, bf16[512,896]{1,0:T(8,128)(2,1)} %doc.4, bf16[256,896]{1,0:T(8,128)(2,1)} %query.3, s32[1,512]{1,0:T(1,128)} %ids.1), custom_call_target="tpu_custom_call" | custom-call | flops 1024 | bytes 1024 | tf_op jit(solution)/shard_map/pallas_call | solution.py:128
  25.5 0.6 gather_fusion
  26.1 0.6 concatenate.34.s
  26.7 0.6 concatenate.35.s
  27.4 0.6 concatenate.36.s
  28.1 33.4 %collective-permute-done.4 = bf16[1024,256]{1,0:T(8,128)(2,1)S(1)} collective-permute-done((bf16[1024,256]{1,0:T(8,128)(2,1)}, bf16[1024,256]{1,0:T(8,128)(2,1)S(1)}, u32[]{:S(2)}, u32[]{:S(2)}) %collective-permute-start.4) | collective-permute-done | bytes 524320 | tf_op jit(solution)/shard_map/ppermute | solution.py:58
  61.5 1.7 collective-permute-done.2.refs_1_.below
  63.2 2.3 collective-permute-done.3.refs_2_.above
  65.5 1.3 collective-permute-start.7
  66.9 2.0 collective-permute-start.8
  68.9 0.2 collective-permute-start.5
  69.1 3.4 %collective-permute-start.6 = (bf16[1024,640]{1,0:T(8,128)(2,1)}, bf16[1024,640]{1,0:T(8,128)(2,1)}, u32[]{:S(2)}, u32[]{:S(2)}) collective-permute-start(bf16[1024,640]{1,0:T(8,128)(2,1)} %collective-permute-done.refs_3_), channel_id=1, source_target_pairs={{0,96},{1,97},{4,100},{5,101},{8,104},{9,105},{12,108},{13,109},{1... | collective-permute-start | bytes 3932168 | tf_op jit(solution)/shard_map/ppermute | solution.py:58
  72.4 0.3 all-gather.4.cloned.1.call-done.refs_3_.refs_6_.refs_8_
  72.7 2.3 shard_map.85.mine
  75.0 1.6 collective-permute-start.9
  76.6 2.2 shard_map.87
  78.9 9.9 %shard_map.84.refs_16_ = f32[768,896]{1,0:T(8,128)} custom-call(s32[32]{0:T(128)} %concatenate.34.s, bf16[1024,640]{1,0:T(8,128)(2,1)} %get-tuple-element.68.refs_0_, bf16[1024,640]{1,0:T(8,128)(2,1)} %copy-done.8, bf16[1024,640]{1,0:T(8,128)(2,1)} %copy-done.9, bf16[6144,256]{1,0:T(8,128)(2,1)} %all-gather.4.cloned.1.call-done.refs_3_.refs_6_.refs_8_, ...), custom_call_target="tpu_custom_call" | custom-call | flops 1024 | bytes 1024 | tf_op jit(solution)/shard_map/pallas_call | solution.py:336
  88.7 11.6 %collective-permute-done.9.theirs = bf16[64,8192]{1,0:T(8,128)(2,1)S(1)} collective-permute-done((bf16[64,8192]{1,0:T(8,128)(2,1)}, bf16[64,8192]{1,0:T(8,128)(2,1)S(1)}, u32[]{:S(2)}, u32[]{:S(2)}) %collective-permute-start.9) | collective-permute-done | bytes 1048608 | tf_op jit(solution)/shard_map/ppermute | solution.py:58
  100.3 1.0 copy-done.15
  101.3 8.6 %shard_map.86 = bf16[128,512]{1,0:T(8,128)(2,1)} custom-call(bf16[64,8192]{1,0:T(8,128)(2,1)} %shard_map.85.mine, bf16[64,8192]{1,0:T(8,128)(2,1)} %copy-done.15, bf16[512,8192]{1,0:T(8,128)(2,1)} %refs_10_.3), custom_call_target="tpu_custom_call" | custom-call | flops 1024 | bytes 1024 | tf_op jit(solution)/shard_map/pallas_call | solution.py:396
  109.9 1.8 collective-permute-done.5.below.refs_4_
  111.7 2.2 collective-permute-done.6.above.refs_5_
  114.1 0.5 collective-permute-start.11
  114.7 3.0 %shard_map.88 = (bf16[2,512,640]{2,1,0:T(8,128)(2,1)}, bf16[2,512,640]{2,1,0:T(8,128)(2,1)}, bf16[384,1024]{1,0:T(8,128)(2,1)}, bf16[384,1024]{1,0:T(8,128)(2,1)}) custom-call(bf16[1024,640]{1,0:T(8,128)(2,1)} %collective-permute-done.5.below.refs_4_, ...), custom_call_target="tpu_custom_call", output_to_operand_aliasing={{0}: (4, {}), {1}: (5, {})} | custom-call | flops 1024 | bytes 1024 | tf_op jit(solution)/shard_map/pallas_call | solution.py:162
  117.7 3.7 %collective-permute-start.16 = (bf16[1024,640]{1,0:T(8,128)(2,1)}, bf16[1024,640]{1,0:T(8,128)(2,1)}, u32[]{:S(2)}, u32[]{:S(2)}) collective-permute-start(bf16[1024,640]{1,0:T(8,128)(2,1)} %bitcast.44), channel_id=1, source_target_pairs={{0,96},{1,97},{4,100},{5,101},{8,104},{9,105},{12,108},{13,109},{1... | collective-permute-start | bytes 3932168 | tf_op jit(solution)/shard_map/ppermute | solution.py:58
  121.5 1.3 collective-permute-start.17
  122.7 0.3 collective-permute-start.13
  123.1 2.9 %collective-permute-start.14 = (bf16[384,1024]{1,0:T(8,128)(2,1)}, bf16[384,1024]{1,0:T(8,128)(2,1)}, u32[]{:S(2)}, u32[]{:S(2)}) collective-permute-start(bf16[384,1024]{1,0:T(8,128)(2,1)} %get-tuple-element.94), channel_id=1, source_target_pairs={{0,12},{1,13},{4,0},{5,1},{8,4},{9,5},{12,8},{13,9},{16,28},{17,29... | collective-permute-start | bytes 2359304 | tf_op jit(solution)/shard_map/ppermute | solution.py:58
  126.0 19.1 %shard_map.89 = (f32[768,896]{1,0:T(8,128)}, f32[768,896]{1,0:T(8,128)}) custom-call(s32[64]{0:T(128)} %concatenate.35.s, bf16[1024,640]{1,0:T(8,128)(2,1)} %get-tuple-element.68.refs_0_, bf16[1024,640]{1,0:T(8,128)(2,1)} %copy-done.8, bf16[1024,640]{1,0:T(8,128)(2,1)} %copy-done.9, bf16[1024,640]{1,0:T(8,128)(2,1)} %collective-permute-done.refs_3_, ...), custom_call_target="tpu_custom_call" | custom-call | flops 1024 | bytes 1024 | tf_op jit(solution)/shard_map/pallas_call | solution.py:336
  145.1 6.0 %collective-permute-done.15.refs_6_ = bf16[1024,640]{1,0:T(8,128)(2,1)} collective-permute-done((bf16[1024,640]{1,0:T(8,128)(2,1)}, bf16[1024,640]{1,0:T(8,128)(2,1)}, u32[]{:S(2)}, u32[]{:S(2)}) %collective-permute-start.15) | collective-permute-done | bytes 1310752 | tf_op jit(solution)/shard_map/ppermute | solution.py:58
  151.2 0.5 collective-permute-start.19
  151.7 2.0 collective-permute-done.18.refs_20_
  153.6 1.1 collective-permute-done.19.refs_21_
  154.8 0.9 copy-done.14
  155.7 10.1 %shard_map.90 = (bf16[256,896]{1,0:T(8,128)(2,1)}, bf16[256,896]{1,0:T(8,128)(2,1)}) custom-call(s32[64]{0:T(128)} %concatenate.36.s, bf16[1024,640]{1,0:T(8,128)(2,1)} %get-tuple-element.68.refs_0_, bf16[1024,640]{1,0:T(8,128)(2,1)} %copy-done.8, bf16[1024,640]{1,0:T(8,128)(2,1)} %copy-done.9, bf16[1024,640]{1,0:T(8,128)(2,1)} %collective-permute-done.refs_3_, ...), custom_call_target="tpu_custom_call" | custom-call | flops 1024 | bytes 1024 | tf_op jit(solution)/shard_map/pallas_call | solution.py:336
  165.8 2.2 collective-permute-start.20
  168.0 1.6 collective-permute-start.21
  169.5 1.7 collective-permute-start.22
  171.3 0.4 copy.13.refs_8_.refs_4_
  171.7 14.2 %shard_map.91.refs_6_.refs_2_ = bf16[1024,896]{1,0:T(8,128)(2,1)} custom-call(s32[64]{0:T(128)} %concatenate.36.s, bf16[1024,640]{1,0:T(8,128)(2,1)} %get-tuple-element.68.refs_0_, bf16[1024,640]{1,0:T(8,128)(2,1)} %copy-done.8, bf16[1024,640]{1,0:T(8,128)(2,1)} %copy-done.9, bf16[1024,640]{1,0:T(8,128)(2,1)} %collective-permute-done.refs_3_, ...), custom_call_target="tpu_custom_call" | custom-call | flops 1024 | bytes 1024 | tf_op jit(solution)/shard_map/pallas_call | solution.py:336
  185.9 3.9 %collective-permute-done.21.refs_3_ = bf16[256,896]{1,0:T(8,128)(2,1)S(1)} collective-permute-done((bf16[256,896]{1,0:T(8,128)(2,1)}, bf16[256,896]{1,0:T(8,128)(2,1)S(1)}, u32[]{:S(2)}, u32[]{:S(2)}) %collective-permute-start.21) | collective-permute-done | bytes 458784 | tf_op jit(solution)/shard_map/ppermute | solution.py:58
  189.8 1.8 collective-permute-done.23.refs_5_
  191.6 0.8 collective-permute-start.24
  192.4 2.4 %collective-permute-start.25 = (bf16[256,896]{1,0:T(8,128)(2,1)S(1)}, bf16[256,896]{1,0:T(8,128)(2,1)}, u32[]{:S(2)}, u32[]{:S(2)}) collective-permute-start(bf16[256,896]{1,0:T(8,128)(2,1)S(1)} %collective-permute-done.23.refs_5_), channel_id=1, source_target_pairs={{0,96},{1,97},{4,100},{5,101},{8,104},{9,105},{12,108},{13,109},{1... | collective-permute-start | bytes 1376264 | tf_op jit(solution)/shard_map/ppermute | solution.py:58
  194.9 2.2 copy-done.2
  197.1 1.5 copy-done.4
  198.6 8.8 %shard_map.92.refs_6_ = f32[32,8]{1,0:T(8,128)S(1)} custom-call(s32[2]{0:T(128)S(1)} %pad_add_fusion.7.s, bf16[256,896]{1,0:T(8,128)(2,1)S(1)} %copy-done.6, bf16[256,896]{1,0:T(8,128)(2,1)S(1)} %copy-done.7, bf16[256,896]{1,0:T(8,128)(2,1)S(1)} %collective-permute-done.20.refs_2_, bf16[256,896]{1,0:T(8,128)(2,1)S(1)} %collective-permute-done.21.refs_3_, ...), custom_call_target="tpu_custom_call" | custom-call | flops 1024 | bytes 1024 | tf_op jit(solution)/shard_map/pallas_call | solution.py:459
  207.5 4.2 %shard_map.93 = f32[32,8]{1,0:T(8,128)S(1)} custom-call(s32[2]{0:T(128)S(1)} %pad_add_fusion.7.s, bf16[256,896]{1,0:T(8,128)(2,1)} %collective-permute-done.24.refs_0_, bf16[256,896]{1,0:T(8,128)(2,1)} %collective-permute-done.25.refs_1_, bf16[1024,896]{1,0:T(8,128)(2,1)S(1)} %copy-done.5, bf16[4,4,2,2,4,16,512]{6,5,4,3,2,1,0:T(8,128)(2,1)S(1)} %bitcast.41, ...), custom_call_target="tpu_custom_call" | custom-call | flops 1024 | bytes 1024 | tf_op jit(solution)/shard_map/pallas_call | solution.py:459
  211.8 1.2 collective-permute-done.26
  212.9 3.7 %collective-permute-done.27 = f32[32,8]{1,0:T(8,128)S(1)} collective-permute-done((f32[32,8]{1,0:T(8,128)S(1)}, f32[32,8]{1,0:T(8,128)S(1)}, u32[]{:S(2)}, u32[]{:S(2)}) %collective-permute-start.27) | collective-permute-done | bytes 1056 | tf_op jit(solution)/shard_map/ppermute | solution.py:58
  216.7 1.3 collective-permute-start.28
  217.9 3.7 %collective-permute-done.28 = f32[32,8]{1,0:T(8,128)S(1)} collective-permute-done((f32[32,8]{1,0:T(8,128)S(1)}, f32[32,8]{1,0:T(8,128)S(1)}, u32[]{:S(2)}, u32[]{:S(2)}) %collective-permute-start.28) | collective-permute-done | bytes 1056 | tf_op jit(solution)/shard_map/ppermute | solution.py:58
  221.6 1.5 collective-permute-start.29
  223.2 2.2 collective-permute-done.29
  225.4 2.5 %collective-permute-start.30 = (f32[32,8]{1,0:T(8,128)S(1)}, f32[32,8]{1,0:T(8,128)S(1)}, u32[]{:S(2)}, u32[]{:S(2)}) collective-permute-start(f32[32,8]{1,0:T(8,128)S(1)} %add.393), channel_id=1, source_target_pairs={{0,18},{1,19},{4,22},{5,23},{8,26},{9,27},{12,30},{13,31},{16,2},{... | collective-permute-start | bytes 3080 | tf_op jit(solution)/shard_map/ppermute | solution.py:58
  227.9 2.4 %collective-permute-done.30 = f32[32,8]{1,0:T(8,128)S(1)} collective-permute-done((f32[32,8]{1,0:T(8,128)S(1)}, f32[32,8]{1,0:T(8,128)S(1)}, u32[]{:S(2)}, u32[]{:S(2)}) %collective-permute-start.30) | collective-permute-done | bytes 1056 | tf_op jit(solution)/shard_map/ppermute | solution.py:58
  230.4 0.7 copy.14
  (90 shorter events, 1.5 us)
Async XLA Ops:
  6.5 18.9 %copy-start = (s32[8,256]{1,0:T(8,128)S(1)}, s32[8,256]{1,0:T(8,128)}, u32[]{:S(2)}) copy-start(s32[8,256]{1,0:T(8,128)} %param.15) | copy-start | bytes 24580
  6.5 66.2 %all-gather.4.cloned.1.call-start = ((), (), s32[]{:S(2)}) async-start(), calls=%async_computation | async-start | bytes 3932160 | tf_op jit(solution)/shard_map/all_gather | solution.py:514
  12.7 113.2 %all-gather.6.cloned.1.call-start = ((), (), s32[]{:S(2)}) async-start(), calls=%async_computation.1 | async-start | bytes 2621440 | tf_op jit(solution)/shard_map/all_gather | solution.py:525
  12.8 50.4 %collective-permute-start.2 = (bf16[1024,640]{1,0:T(8,128)(2,1)}, bf16[1024,640]{1,0:T(8,128)(2,1)S(1)}, u32[]{:S(2)}, u32[]{:S(2)}) collective-permute-start(bf16[1024,640]{1,0:T(8,128)(2,1)} %get-tuple-element.68.refs_0_), channel_id=1, source_target_pairs={{0,32},{1,33},{4,36},{5,37},{8,40},{9,41},{12,44},{13,45},{16,48},... | collective-permute-start | bytes 3932168 | tf_op jit(solution)/shard_map/ppermute | solution.py:58
  14.9 50.6 %collective-permute-start.3 = (bf16[1024,640]{1,0:T(8,128)(2,1)}, bf16[1024,640]{1,0:T(8,128)(2,1)S(1)}, u32[]{:S(2)}, u32[]{:S(2)}) collective-permute-start(bf16[1024,640]{1,0:T(8,128)(2,1)} %get-tuple-element.68.refs_0_), channel_id=1, source_target_pairs={{0,96},{1,97},{4,100},{5,101},{8,104},{9,105},{12,108},{13,109},{1... | collective-permute-start | bytes 3932168 | tf_op jit(solution)/shard_map/ppermute | solution.py:58
  17.1 48.4 %collective-permute-start.1 = (bf16[768,1024]{1,0:T(8,128)(2,1)}, bf16[768,1024]{1,0:T(8,128)(2,1)}, u32[]{:S(2)}, u32[]{:S(2)}) collective-permute-start(bf16[768,1024]{1,0:T(8,128)(2,1)} %get-tuple-element.67), channel_id=1, source_target_pairs={{0,18},{1,19},{4,22},{5,23},{8,26},{9,27},{12,30},{13,31},{16,2},{... | collective-permute-start | bytes 4718600 | tf_op jit(solution)/shard_map/ppermute | solution.py:58
  20.1 41.4 %collective-permute-start = (bf16[1024,640]{1,0:T(8,128)(2,1)}, bf16[1024,640]{1,0:T(8,128)(2,1)}, u32[]{:S(2)}, u32[]{:S(2)}) collective-permute-start(bf16[1024,640]{1,0:T(8,128)(2,1)} %get-tuple-element.66), channel_id=1, source_target_pairs={{0,16},{1,17},{4,20},{5,21},{8,24},{9,25},{12,28},{13,29},{16,0},{... | collective-permute-start | bytes 3932168 | tf_op jit(solution)/shard_map/ppermute | solution.py:58
  20.2 41.3 %collective-permute-start.4 = (bf16[1024,256]{1,0:T(8,128)(2,1)}, bf16[1024,256]{1,0:T(8,128)(2,1)S(1)}, u32[]{:S(2)}, u32[]{:S(2)}) collective-permute-start(bf16[1024,256]{1,0:T(8,128)(2,1)} %get-tuple-element.69), channel_id=1, source_target_pairs={{0,16},{1,17},{4,20},{5,21},{8,24},{9,25},{12,28},{13,29},{16,0},{... | collective-permute-start | bytes 1572872 | tf_op jit(solution)/shard_map/ppermute | solution.py:58
  61.5 4.0 %copy-start.16 = (bf16[1024,256]{1,0:T(8,128)(2,1)}, bf16[1024,256]{1,0:T(8,128)(2,1)S(1)}, u32[]{:S(2)}) copy-start(bf16[1024,256]{1,0:T(8,128)(2,1)S(1)} %collective-permute-done.4) | copy-start | bytes 1572868
  63.2 11.8 %copy-start.8 = (bf16[1024,640]{1,0:T(8,128)(2,1)}, bf16[1024,640]{1,0:T(8,128)(2,1)S(1)}, u32[]{:S(2)}) copy-start(bf16[1024,640]{1,0:T(8,128)(2,1)S(1)} %collective-permute-done.2.refs_1_.below) | copy-start | bytes 3932164
  65.5 9.5 %copy-start.9 = (bf16[1024,640]{1,0:T(8,128)(2,1)}, bf16[1024,640]{1,0:T(8,128)(2,1)S(1)}, u32[]{:S(2)}) copy-start(bf16[1024,640]{1,0:T(8,128)(2,1)S(1)} %collective-permute-done.3.refs_2_.above) | copy-start | bytes 3932164
  65.5 129.4 %all-gather.8.cloned.1.call-start = ((), (), s32[]{:S(2)}) async-start(), calls=%async_computation.2 | async-start | bytes 4325376 | tf_op jit(solution)/shard_map/all_gather | solution.py:551
  65.5 48.4 %collective-permute-start.7 = (bf16[768,1024]{1,0:T(8,128)(2,1)}, bf16[768,1024]{1,0:T(8,128)(2,1)}, u32[]{:S(2)}, u32[]{:S(2)}) collective-permute-start(bf16[768,1024]{1,0:T(8,128)(2,1)} %collective-permute-done.1.refs_10_.refs_12_), channel_id=1, source_target_pairs={{0,4},{1,5},{4,8},{5,9},{8,12},{9,13},{12,0},{13,1},{16,20},{17,21... | collective-permute-start | bytes 4718600 | tf_op jit(solution)/shard_map/ppermute | solution.py:58
  66.9 47.1 %collective-permute-start.8 = (bf16[768,1024]{1,0:T(8,128)(2,1)}, bf16[768,1024]{1,0:T(8,128)(2,1)}, u32[]{:S(2)}, u32[]{:S(2)}) collective-permute-start(bf16[768,1024]{1,0:T(8,128)(2,1)} %collective-permute-done.1.refs_10_.refs_12_), channel_id=1, source_target_pairs={{0,12},{1,13},{4,0},{5,1},{8,4},{9,5},{12,8},{13,9},{16,28},{17,29... | collective-permute-start | bytes 4718600 | tf_op jit(solution)/shard_map/ppermute | solution.py:58
  68.9 42.9 %collective-permute-start.5 = (bf16[1024,640]{1,0:T(8,128)(2,1)}, bf16[1024,640]{1,0:T(8,128)(2,1)}, u32[]{:S(2)}, u32[]{:S(2)}) collective-permute-start(bf16[1024,640]{1,0:T(8,128)(2,1)} %collective-permute-done.refs_3_), channel_id=1, source_target_pairs={{0,32},{1,33},{4,36},{5,37},{8,40},{9,41},{12,44},{13,45},{16,48},... | collective-permute-start | bytes 3932168 | tf_op jit(solution)/shard_map/ppermute | solution.py:58
  69.1 44.8 %collective-permute-start.6 = (bf16[1024,640]{1,0:T(8,128)(2,1)}, bf16[1024,640]{1,0:T(8,128)(2,1)}, u32[]{:S(2)}, u32[]{:S(2)}) collective-permute-start(bf16[1024,640]{1,0:T(8,128)(2,1)} %collective-permute-done.refs_3_), channel_id=1, source_target_pairs={{0,96},{1,97},{4,100},{5,101},{8,104},{9,105},{12,108},{13,109},{1... | collective-permute-start | bytes 3932168 | tf_op jit(solution)/shard_map/ppermute | solution.py:58
  75.0 25.3 %collective-permute-start.9 = (bf16[64,8192]{1,0:T(8,128)(2,1)}, bf16[64,8192]{1,0:T(8,128)(2,1)S(1)}, u32[]{:S(2)}, u32[]{:S(2)}) collective-permute-start(bf16[64,8192]{1,0:T(8,128)(2,1)} %shard_map.85.mine), channel_id=1, source_target_pairs={{0,16},{1,17},{4,20},{5,21},{8,24},{9,25},{12,28},{13,29},{16,0},{... | collective-permute-start | bytes 3145736 | tf_op jit(solution)/shard_map/ppermute | solution.py:58
  100.3 1.0 copy-start.15
  114.0 7.5 %collective-permute-start.10 = (bf16[768,1024]{1,0:T(8,128)(2,1)}, bf16[768,1024]{1,0:T(8,128)(2,1)S(1)}, u32[]{:S(2)}, u32[]{:S(2)}) collective-permute-start(bf16[768,1024]{1,0:T(8,128)(2,1)} %collective-permute-done.1.refs_10_.refs_12_), channel_id=1, source_target_pairs={{0,1},{1,0},{4,5},{5,4},{8,9},{9,8},{12,13},{13,12},{16,17},{17,16... | collective-permute-start | bytes 4718600 | tf_op jit(solution)/shard_map/ppermute | solution.py:58
  114.1 8.7 %collective-permute-start.11 = (bf16[768,1024]{1,0:T(8,128)(2,1)}, bf16[768,1024]{1,0:T(8,128)(2,1)}, u32[]{:S(2)}, u32[]{:S(2)}) collective-permute-start(bf16[768,1024]{1,0:T(8,128)(2,1)} %collective-permute-done.7.x_below.refs_12_.refs_14_), channel_id=1, source_target_pairs={{0,1},{1,0},{4,5},{5,4},{8,9},{9,8},{12,13},{13,12},{16,17},{17,16... | collective-permute-start | bytes 4718600 | tf_op jit(solution)/shard_map/ppermute | solution.py:58
  114.6 8.2 %collective-permute-start.12 = (bf16[768,1024]{1,0:T(8,128)(2,1)}, bf16[768,1024]{1,0:T(8,128)(2,1)}, u32[]{:S(2)}, u32[]{:S(2)}) collective-permute-start(bf16[768,1024]{1,0:T(8,128)(2,1)} %collective-permute-done.8.x_above.refs_14_.refs_16_), channel_id=1, source_target_pairs={{0,1},{1,0},{4,5},{5,4},{8,9},{9,8},{12,13},{13,12},{16,17},{17,16... | collective-permute-start | bytes 4718600 | tf_op jit(solution)/shard_map/ppermute | solution.py:58
  117.7 33.4 %collective-permute-start.15 = (bf16[1024,640]{1,0:T(8,128)(2,1)}, bf16[1024,640]{1,0:T(8,128)(2,1)}, u32[]{:S(2)}, u32[]{:S(2)}) collective-permute-start(bf16[1024,640]{1,0:T(8,128)(2,1)} %bitcast.43), channel_id=1, source_target_pairs={{0,32},{1,33},{4,36},{5,37},{8,40},{9,41},{12,44},{13,45},{16,48},... | collective-permute-start | bytes 3932168 | tf_op jit(solution)/shard_map/ppermute | solution.py:58
  117.7 33.3 %collective-permute-start.16 = (bf16[1024,640]{1,0:T(8,128)(2,1)}, bf16[1024,640]{1,0:T(8,128)(2,1)}, u32[]{:S(2)}, u32[]{:S(2)}) collective-permute-start(bf16[1024,640]{1,0:T(8,128)(2,1)} %bitcast.44), channel_id=1, source_target_pairs={{0,96},{1,97},{4,100},{5,101},{8,104},{9,105},{12,108},{13,109},{1... | collective-permute-start | bytes 3932168 | tf_op jit(solution)/shard_map/ppermute | solution.py:58
  121.5 4.5 %copy-start.10 = (bf16[768,1024]{1,0:T(8,128)(2,1)}, bf16[768,1024]{1,0:T(8,128)(2,1)S(1)}, u32[]{:S(2)}) copy-start(bf16[768,1024]{1,0:T(8,128)(2,1)S(1)} %collective-permute-done.10.refs_11_.refs_13_) | copy-start | bytes 4718596
  121.5 23.6 %collective-permute-start.17 = (bf16[784,512]{1,0:T(8,128)(2,1)}, bf16[784,512]{1,0:T(8,128)(2,1)S(1)}, u32[]{:S(2)}, u32[]{:S(2)}) collective-permute-start(bf16[784,512]{1,0:T(8,128)(2,1)} %get-tuple-element.105), channel_id=1, source_target_pairs={{0,16},{1,17},{4,20},{5,21},{8,24},{9,25},{12,28},{13,29},{16,0},{... | collective-permute-start | bytes 2408456 | tf_op jit(solution)/shard_map/ppermute | solution.py:58
  122.7 28.3 %collective-permute-start.13 = (bf16[384,1024]{1,0:T(8,128)(2,1)}, bf16[384,1024]{1,0:T(8,128)(2,1)S(1)}, u32[]{:S(2)}, u32[]{:S(2)}) collective-permute-start(bf16[384,1024]{1,0:T(8,128)(2,1)} %get-tuple-element.93), channel_id=1, source_target_pairs={{0,4},{1,5},{4,8},{5,9},{8,12},{9,13},{12,0},{13,1},{16,20},{17,21... | collective-permute-start | bytes 2359304 | tf_op jit(solution)/shard_map/ppermute | solution.py:58
  123.1 28.0 %collective-permute-start.14 = (bf16[384,1024]{1,0:T(8,128)(2,1)}, bf16[384,1024]{1,0:T(8,128)(2,1)}, u32[]{:S(2)}, u32[]{:S(2)}) collective-permute-start(bf16[384,1024]{1,0:T(8,128)(2,1)} %get-tuple-element.94), channel_id=1, source_target_pairs={{0,12},{1,13},{4,0},{5,1},{8,4},{9,5},{12,8},{13,9},{16,28},{17,29... | collective-permute-start | bytes 2359304 | tf_op jit(solution)/shard_map/ppermute | solution.py:58
  145.0 9.7 %copy-start.11 = (bf16[784,512]{1,0:T(8,128)(2,1)}, bf16[784,512]{1,0:T(8,128)(2,1)S(1)}, u32[]{:S(2)}) copy-start(bf16[784,512]{1,0:T(8,128)(2,1)S(1)} %collective-permute-done.17.refs_25_) | copy-start | bytes 2408452
  151.1 3.7 %copy-start.12 = (bf16[384,1024]{1,0:T(8,128)(2,1)}, bf16[384,1024]{1,0:T(8,128)(2,1)S(1)}, u32[]{:S(2)}) copy-start(bf16[384,1024]{1,0:T(8,128)(2,1)S(1)} %collective-permute-done.13.refs_18_) | copy-start | bytes 2359300
  151.1 2.6 %collective-permute-start.18 = (bf16[384,1024]{1,0:T(8,128)(2,1)S(1)}, bf16[384,1024]{1,0:T(8,128)(2,1)S(1)}, u32[]{:S(2)}, u32[]{:S(2)}) collective-permute-start(bf16[384,1024]{1,0:T(8,128)(2,1)S(1)} %collective-permute-done.13.refs_18_), channel_id=1, source_target_pairs={{0,1},{1,0},{4,5},{5,4},{8,9},{9,8},{12,13},{13,12},{16,17},{17,16... | collective-permute-start | bytes 2359304 | tf_op jit(solution)/shard_map/ppermute | solution.py:58
  151.2 3.6 %collective-permute-start.19 = (bf16[384,1024]{1,0:T(8,128)(2,1)}, bf16[384,1024]{1,0:T(8,128)(2,1)S(1)}, u32[]{:S(2)}, u32[]{:S(2)}) collective-permute-start(bf16[384,1024]{1,0:T(8,128)(2,1)} %collective-permute-done.14.refs_19_), channel_id=1, source_target_pairs={{0,1},{1,0},{4,5},{5,4},{8,9},{9,8},{12,13},{13,12},{16,17},{17,16... | collective-permute-start | bytes 2359304 | tf_op jit(solution)/shard_map/ppermute | solution.py:58
  153.6 1.2 copy-start.13
  154.8 0.9 copy-start.14
  165.8 20.1 %collective-permute-start.20 = (bf16[256,896]{1,0:T(8,128)(2,1)}, bf16[256,896]{1,0:T(8,128)(2,1)S(1)}, u32[]{:S(2)}, u32[]{:S(2)}) collective-permute-start(bf16[256,896]{1,0:T(8,128)(2,1)} %get-tuple-element.116.refs_0_), channel_id=1, source_target_pairs={{0,32},{1,33},{4,36},{5,37},{8,40},{9,41},{12,44},{13,45},{16,48},... | collective-permute-start | bytes 1376264 | tf_op jit(solution)/shard_map/ppermute | solution.py:58
  168.0 21.8 %collective-permute-start.21 = (bf16[256,896]{1,0:T(8,128)(2,1)}, bf16[256,896]{1,0:T(8,128)(2,1)S(1)}, u32[]{:S(2)}, u32[]{:S(2)}) collective-permute-start(bf16[256,896]{1,0:T(8,128)(2,1)} %get-tuple-element.117.refs_1_), channel_id=1, source_target_pairs={{0,32},{1,33},{4,36},{5,37},{8,40},{9,41},{12,44},{13,45},{16,48},... | collective-permute-start | bytes 1376264 | tf_op jit(solution)/shard_map/ppermute | solution.py:58
  169.5 20.2 %collective-permute-start.22 = (bf16[256,896]{1,0:T(8,128)(2,1)}, bf16[256,896]{1,0:T(8,128)(2,1)}, u32[]{:S(2)}, u32[]{:S(2)}) collective-permute-start(bf16[256,896]{1,0:T(8,128)(2,1)} %get-tuple-element.116.refs_0_), channel_id=1, source_target_pairs={{0,96},{1,97},{4,100},{5,101},{8,104},{9,105},{12,108},{13,109},{1... | collective-permute-start | bytes 1376264 | tf_op jit(solution)/shard_map/ppermute | solution.py:58
  171.2 20.4 %collective-permute-start.23 = (bf16[256,896]{1,0:T(8,128)(2,1)}, bf16[256,896]{1,0:T(8,128)(2,1)S(1)}, u32[]{:S(2)}, u32[]{:S(2)}) collective-permute-start(bf16[256,896]{1,0:T(8,128)(2,1)} %get-tuple-element.117.refs_1_), channel_id=1, source_target_pairs={{0,96},{1,97},{4,100},{5,101},{8,104},{9,105},{12,108},{13,109},{1... | collective-permute-start | bytes 1376264 | tf_op jit(solution)/shard_map/ppermute | solution.py:58
  171.6 23.2 %copy-start.17 = (s32[1,512]{1,0:T(1,128)S(1)}, s32[1,512]{1,0:T(1,128)}, u32[]{:S(2)}) copy-start(s32[1,512]{1,0:T(1,128)} %ids.1) | copy-start | bytes 6148
  171.6 23.3 %copy-start.6 = (bf16[256,896]{1,0:T(8,128)(2,1)S(1)}, bf16[256,896]{1,0:T(8,128)(2,1)}, u32[]{:S(2)}) copy-start(bf16[256,896]{1,0:T(8,128)(2,1)} %get-tuple-element.116.refs_0_) | copy-start | bytes 1376260
  171.6 23.3 %copy-start.7 = (bf16[256,896]{1,0:T(8,128)(2,1)S(1)}, bf16[256,896]{1,0:T(8,128)(2,1)}, u32[]{:S(2)}) copy-start(bf16[256,896]{1,0:T(8,128)(2,1)} %get-tuple-element.117.refs_1_) | copy-start | bytes 1376260
  191.6 15.8 %collective-permute-start.24 = (bf16[256,896]{1,0:T(8,128)(2,1)S(1)}, bf16[256,896]{1,0:T(8,128)(2,1)}, u32[]{:S(2)}, u32[]{:S(2)}) collective-permute-start(bf16[256,896]{1,0:T(8,128)(2,1)S(1)} %collective-permute-done.20.refs_2_), channel_id=1, source_target_pairs={{0,32},{1,33},{4,36},{5,37},{8,40},{9,41},{12,44},{13,45},{16,48},... | collective-permute-start | bytes 1376264 | tf_op jit(solution)/shard_map/ppermute | solution.py:58
  192.4 15.0 %collective-permute-start.25 = (bf16[256,896]{1,0:T(8,128)(2,1)S(1)}, bf16[256,896]{1,0:T(8,128)(2,1)}, u32[]{:S(2)}, u32[]{:S(2)}) collective-permute-start(bf16[256,896]{1,0:T(8,128)(2,1)S(1)} %collective-permute-done.23.refs_5_), channel_id=1, source_target_pairs={{0,96},{1,97},{4,100},{5,101},{8,104},{9,105},{12,108},{13,109},{1... | collective-permute-start | bytes 1376264 | tf_op jit(solution)/shard_map/ppermute | solution.py:58
  194.9 2.2 copy-start.2
  197.1 1.5 copy-start.4
  198.6 8.8 %copy-start.3 = (bf16[4096,512]{1,0:T(8,128)(2,1)S(1)}, bf16[4096,512]{1,0:T(8,128)(2,1)}, u32[]{:S(2)}) copy-start(bf16[4096,512]{1,0:T(8,128)(2,1)} %all-gather.8.cloned.1.call-done) | copy-start | bytes 12582916
  198.6 8.8 %copy-start.5 = (bf16[1024,896]{1,0:T(8,128)(2,1)S(1)}, bf16[1024,896]{1,0:T(8,128)(2,1)}, u32[]{:S(2)}) copy-start(bf16[1024,896]{1,0:T(8,128)(2,1)} %shard_map.91.refs_6_.refs_2_) | copy-start | bytes 5505028
  207.5 23.6 %copy-start.1 = (s32[8,256]{1,0:T(8,128)S(1)}, s32[8,256]{1,0:T(8,128)}, u32[]{:S(2)}) copy-start(s32[8,256]{1,0:T(8,128)} %param.15) | copy-start | bytes 24580
  211.7 1.3 collective-permute-start.26
  212.9 3.7 %collective-permute-start.27 = (f32[32,8]{1,0:T(8,128)S(1)}, f32[32,8]{1,0:T(8,128)S(1)}, u32[]{:S(2)}, u32[]{:S(2)}) collective-permute-start(f32[32,8]{1,0:T(8,128)S(1)} %add.390), channel_id=1, source_target_pairs={{0,4},{1,5},{4,0},{5,1},{8,12},{9,13},{12,8},{13,9},{16,20},{17,21... | collective-permute-start | bytes 3080 | tf_op jit(solution)/shard_map/ppermute | solution.py:58
  216.7 4.9 %collective-permute-start.28 = (f32[32,8]{1,0:T(8,128)S(1)}, f32[32,8]{1,0:T(8,128)S(1)}, u32[]{:S(2)}, u32[]{:S(2)}) collective-permute-start(f32[32,8]{1,0:T(8,128)S(1)} %add.391), channel_id=1, source_target_pairs={{0,12},{1,13},{4,8},{5,9},{8,4},{9,5},{12,0},{13,1},{16,28},{17,29... | collective-permute-start | bytes 3080 | tf_op jit(solution)/shard_map/ppermute | solution.py:58
  221.6 3.7 %collective-permute-start.29 = (f32[32,8]{1,0:T(8,128)S(1)}, f32[32,8]{1,0:T(8,128)S(1)}, u32[]{:S(2)}, u32[]{:S(2)}) collective-permute-start(f32[32,8]{1,0:T(8,128)S(1)} %add.392), channel_id=1, source_target_pairs={{0,16},{1,17},{4,20},{5,21},{8,24},{9,25},{12,28},{13,29},{16,0},{... | collective-permute-start | bytes 3080 | tf_op jit(solution)/shard_map/ppermute | solution.py:58
  225.4 4.9 %collective-permute-start.30 = (f32[32,8]{1,0:T(8,128)S(1)}, f32[32,8]{1,0:T(8,128)S(1)}, u32[]{:S(2)}, u32[]{:S(2)}) collective-permute-start(f32[32,8]{1,0:T(8,128)S(1)} %add.393), channel_id=1, source_target_pairs={{0,18},{1,19},{4,22},{5,23},{8,26},{9,27},{12,30},{13,31},{16,2},{... | collective-permute-start | bytes 3080 | tf_op jit(solution)/shard_map/ppermute | solution.py:58
Sparse Core Ops, SparseCore 0:
  12.9 59.8 all-gather.3
  74.4 42.1 all-gather.5
  118.8 48.2 all-gather.7

commit v2 on v1

--- a/solution.py
+++ b/solution.py
@@ -563,10 +563,11 @@
     lower, upper = jnp.where(ylo == 0, doc_ids, ids_too), jnp.where(ylo == 0, ids_too, doc_ids)
     both = jnp.concatenate([lower, upper + DOCS], 1)
     docs = (both == jnp.arange(2 * DOCS, dtype=jnp.int32)[:, None]).astype(F32)
-    q_below, q_above = [send(v, ZP) for v in q], [send(v, ZM) for v in q]
+    q_below, q_above = [send(v, ZP) for v in q], [send(v, ZM) for v in q[::-1]][::-1]
     (d,) = factors(rest, late, all_w, thins, own, all_x, (own_part, other_part), grads, (0, TOK))
-    *around, d = tie(*q_below, *q_above, d)
-    q_far0, q_far1 = send(around[0], ZP), send(around[3], ZM)
+    q_below[0], q_above[1], d = tie(q_below[0], q_above[1], d)
+    q_far0, q_far1 = send(q_below[0], ZP), send(q_above[1], ZM)
+    around = (*q_below, *q_above)
 
     scores = jnp.zeros((8 * QS, 2 * DOCS), F32)
     scores = score_sums(0, where, (*q, *around), d, gram, ids, docs, scores)

time: 238 us -> 235 us (0.987)
  waiting for transfers between devices: 81.5 us -> 77.7 us
    ppermute x31, waiting for transfers between devices: 81.1 us -> 77.3 us  [send(): return lax.ppermute(v, AX, p)]
    unnamed x37 -> x41, local copies, waits for them, and re-layouts: 5.63 us -> 7.4 us
  transfers between devices with their start and end apart: 34 -> 34, of which waited for: 17 -> 16; matrix products, arithmetic and copies ran while one was open for 1% -> 2% of each run, Pallas kernels for 34% -> 34%
where the time goes in v2:
time: 235 us
  Pallas kernels  89.1 us (38%)
  waiting for transfers between devices  77.7 us (33%)
  starting transfers between devices  42 us (18%)
  between operations  13.5 us (6%)
  local copies, waits for them, and re-layouts  11.1 us (5%)
    ppermute x31, waiting for transfers between devices, send(): return lax.ppermute(v, AX, p)  77.3 us
    pallas_call x4, Pallas kernels, factors(): pl.pallas_call(functools.partial(factor_kernel, phases, m, row, split, le...  53 us
    ppermute x31, starting transfers between devices, send(): return lax.ppermute(v, AX, p)  41.9 us
    pallas_call x2, Pallas kernels, score_sums(): pl.pallas_call(functools.partial(score_kernel, first, len(queries) // 2),...  11.7 us
    pallas_call x1, Pallas kernels, gram_part(): pl.pallas_call(gram_kernel, grid=(8,), in_specs=[few, few, pl.BlockSpec((...  8.56 us
    unnamed x41, local copies, waits for them, and re-layouts  7.4 us
    pallas_call x1, Pallas kernels, pack(): pl.pallas_call(pack_kernel, grid_spec=pltpu.PrefetchScalarGridSpec(num_sc...  5.56 us
    pallas_call x2, Pallas kernels, halves(): pl.pallas_call(halves_b_kernel if into else halves_a_kernel, grid=(steps,...  5.2 us
  transfers between devices with their start and end apart: 34, of which 16 were waited for; matrix products, arithmetic and copies ran while one was open for 2% of the time, Pallas kernels for 34%

profile of v2, /device:TPU:0, one launch (start us, length us, event | category | flops | bytes accessed | tf_op | source)
XLA Modules:
  0.0 234.6 jit_solution(653348430562835409)
XLA Ops:
  6.5 0.6 pad_add_fusion.1.s
  7.1 5.6 %shard_map.82 = (bf16[1024,640]{1,0:T(8,128)(2,1)}, bf16[1536,256]{1,0:T(8,128)(2,1)}, bf16[1024,640]{1,0:T(8,128)(2,1)}, bf16[1024,256]{1,0:T(8,128)(2,1)}, bf16[768,1024]{1,0:T(8,128)(2,1)}) custom-call(s32[3]{0:T(128)} %pad_add_fusion.1.s, bf16[1024,896]{1,0:T(8,128)(2,1)} %gate.1, bf16[1024,896]{1,0:T(8,128)(2,1)} %up.1, bf16[512,8192]{1,0:T(8,128)(2,1)} %refs_10_.3, ...), custom_call_target="tpu_custom_call" | custom-call | flops 1024 | bytes 1024 | tf_op jit(solution)/shard_map/pallas_call | solution.py:99
  12.8 2.1 collective-permute-start.2
  14.8 2.2 collective-permute-start.3
  17.1 3.0 %collective-permute-start.1 = (bf16[768,1024]{1,0:T(8,128)(2,1)}, bf16[768,1024]{1,0:T(8,128)(2,1)}, u32[]{:S(2)}, u32[]{:S(2)}) collective-permute-start(bf16[768,1024]{1,0:T(8,128)(2,1)} %get-tuple-element.65), channel_id=1, source_target_pairs={{0,18},{1,19},{4,22},{5,23},{8,26},{9,27},{12,30},{13,31},{16,2},{... | collective-permute-start | bytes 4718600 | tf_op jit(solution)/shard_map/ppermute | solution.py:58
  20.2 1.9 collective-permute-start.4
  22.2 2.8 %shard_map.83 = (bf16[768,512]{1,0:T(8,128)(2,1)}, bf16[784,512]{1,0:T(8,128)(2,1)}) custom-call(s32[1]{0:T(128)} %bitcast.ylo_ref, bf16[512,896]{1,0:T(8,128)(2,1)} %doc.4, bf16[256,896]{1,0:T(8,128)(2,1)} %query.3, s32[1,512]{1,0:T(1,128)} %ids.1), custom_call_target="tpu_custom_call" | custom-call | flops 1024 | bytes 1024 | tf_op jit(solution)/shard_map/pallas_call | solution.py:128
  25.4 0.6 gather_fusion
  26.0 0.6 concatenate.34.s
  26.6 0.7 concatenate.35.s
  27.4 0.7 concatenate.36.s
  28.2 33.3 %collective-permute-done.4 = bf16[1024,256]{1,0:T(8,128)(2,1)S(1)} collective-permute-done((bf16[1024,256]{1,0:T(8,128)(2,1)}, bf16[1024,256]{1,0:T(8,128)(2,1)S(1)}, u32[]{:S(2)}, u32[]{:S(2)}) %collective-permute-start.4) | collective-permute-done | bytes 524320 | tf_op jit(solution)/shard_map/ppermute | solution.py:58
  61.5 1.7 collective-permute-done.2.refs_1_.below
  63.2 2.3 collective-permute-done.3.refs_2_.above
  65.5 1.3 collective-permute-start.7
  66.9 2.0 collective-permute-start.8
  68.8 0.2 collective-permute-start.5
  69.1 3.4 %collective-permute-start.6 = (bf16[1024,640]{1,0:T(8,128)(2,1)}, bf16[1024,640]{1,0:T(8,128)(2,1)}, u32[]{:S(2)}, u32[]{:S(2)}) collective-permute-start(bf16[1024,640]{1,0:T(8,128)(2,1)} %collective-permute-done.refs_3_), channel_id=1, source_target_pairs={{0,96},{1,97},{4,100},{5,101},{8,104},{9,105},{12,108},{13,109},{1... | collective-permute-start | bytes 3932168 | tf_op jit(solution)/shard_map/ppermute | solution.py:58
  72.4 0.3 all-gather.4.cloned.1.call-done.refs_3_.refs_6_.refs_8_
  72.7 2.3 shard_map.85.mine
  75.0 1.6 collective-permute-start.9
  76.6 2.2 shard_map.87
  78.8 9.8 %shard_map.84.refs_16_ = f32[768,896]{1,0:T(8,128)} custom-call(s32[32]{0:T(128)} %concatenate.34.s, bf16[1024,640]{1,0:T(8,128)(2,1)} %get-tuple-element.66.refs_0_, bf16[1024,640]{1,0:T(8,128)(2,1)} %copy-done.10, bf16[1024,640]{1,0:T(8,128)(2,1)} %copy-done.11, bf16[6144,256]{1,0:T(8,128)(2,1)} %all-gather.4.cloned.1.call-done.refs_3_.refs_6_.refs_8_, ...), custom_call_target="tpu_custom_call" | custom-call | flops 1024 | bytes 1024 | tf_op jit(solution)/shard_map/pallas_call | solution.py:336
  88.7 11.6 %collective-permute-done.9.theirs = bf16[64,8192]{1,0:T(8,128)(2,1)S(1)} collective-permute-done((bf16[64,8192]{1,0:T(8,128)(2,1)}, bf16[64,8192]{1,0:T(8,128)(2,1)S(1)}, u32[]{:S(2)}, u32[]{:S(2)}) %collective-permute-start.9) | collective-permute-done | bytes 1048608 | tf_op jit(solution)/shard_map/ppermute | solution.py:58
  100.3 1.0 copy-done.17
  101.3 8.6 %shard_map.86 = bf16[128,512]{1,0:T(8,128)(2,1)} custom-call(bf16[64,8192]{1,0:T(8,128)(2,1)} %shard_map.85.mine, bf16[64,8192]{1,0:T(8,128)(2,1)} %copy-done.17, bf16[512,8192]{1,0:T(8,128)(2,1)} %refs_10_.3), custom_call_target="tpu_custom_call" | custom-call | flops 1024 | bytes 1024 | tf_op jit(solution)/shard_map/pallas_call | solution.py:396
  109.8 1.9 collective-permute-done.5.below.refs_4_
  111.7 2.2 collective-permute-done.6.above.refs_5_
  114.1 0.5 collective-permute-start.11
  114.6 3.0 %shard_map.88 = (bf16[2,512,640]{2,1,0:T(8,128)(2,1)}, bf16[2,512,640]{2,1,0:T(8,128)(2,1)}, bf16[384,1024]{1,0:T(8,128)(2,1)}, bf16[384,1024]{1,0:T(8,128)(2,1)}) custom-call(bf16[1024,640]{1,0:T(8,128)(2,1)} %collective-permute-done.5.below.refs_4_, ...), custom_call_target="tpu_custom_call", output_to_operand_aliasing={{0}: (4, {}), {1}: (5, {})} | custom-call | flops 1024 | bytes 1024 | tf_op jit(solution)/shard_map/pallas_call | solution.py:162
  117.7 3.7 %collective-permute-start.16 = (bf16[1024,640]{1,0:T(8,128)(2,1)}, bf16[1024,640]{1,0:T(8,128)(2,1)}, u32[]{:S(2)}, u32[]{:S(2)}) collective-permute-start(bf16[1024,640]{1,0:T(8,128)(2,1)} %bitcast.44), channel_id=1, source_target_pairs={{0,96},{1,97},{4,100},{5,101},{8,104},{9,105},{12,108},{13,109},{1... | collective-permute-start | bytes 3932168 | tf_op jit(solution)/shard_map/ppermute | solution.py:58
  121.4 1.3 collective-permute-start.17
  122.7 0.3 collective-permute-start.13
  123.0 2.9 %collective-permute-start.14 = (bf16[384,1024]{1,0:T(8,128)(2,1)}, bf16[384,1024]{1,0:T(8,128)(2,1)}, u32[]{:S(2)}, u32[]{:S(2)}) collective-permute-start(bf16[384,1024]{1,0:T(8,128)(2,1)} %get-tuple-element.92), channel_id=1, source_target_pairs={{0,12},{1,13},{4,0},{5,1},{8,4},{9,5},{12,8},{13,9},{16,28},{17,29... | collective-permute-start | bytes 2359304 | tf_op jit(solution)/shard_map/ppermute | solution.py:58
  125.9 19.1 %shard_map.89 = (f32[768,896]{1,0:T(8,128)}, f32[768,896]{1,0:T(8,128)}) custom-call(s32[64]{0:T(128)} %concatenate.35.s, bf16[1024,640]{1,0:T(8,128)(2,1)} %get-tuple-element.66.refs_0_, bf16[1024,640]{1,0:T(8,128)(2,1)} %copy-done.10, bf16[1024,640]{1,0:T(8,128)(2,1)} %copy-done.11, bf16[1024,640]{1,0:T(8,128)(2,1)} %collective-permute-done.refs_3_, ...), custom_call_target="tpu_custom_call" | custom-call | flops 1024 | bytes 1024 | tf_op jit(solution)/shard_map/pallas_call | solution.py:336
  145.0 6.0 %collective-permute-done.15.refs_6_ = bf16[1024,640]{1,0:T(8,128)(2,1)} collective-permute-done((bf16[1024,640]{1,0:T(8,128)(2,1)}, bf16[1024,640]{1,0:T(8,128)(2,1)}, u32[]{:S(2)}, u32[]{:S(2)}) %collective-permute-start.15) | collective-permute-done | bytes 1310752 | tf_op jit(solution)/shard_map/ppermute | solution.py:58
  151.1 0.5 collective-permute-start.19
  151.6 2.0 collective-permute-done.18.refs_20_
  153.6 1.1 collective-permute-done.19.refs_21_
  154.7 0.9 copy-done.16
  155.6 10.1 %shard_map.90 = (bf16[256,896]{1,0:T(8,128)(2,1)}, bf16[256,896]{1,0:T(8,128)(2,1)}) custom-call(s32[64]{0:T(128)} %concatenate.36.s, bf16[1024,640]{1,0:T(8,128)(2,1)} %get-tuple-element.66.refs_0_, bf16[1024,640]{1,0:T(8,128)(2,1)} %copy-done.10, bf16[1024,640]{1,0:T(8,128)(2,1)} %copy-done.11, bf16[1024,640]{1,0:T(8,128)(2,1)} %collective-permute-done.refs_3_, ...), custom_call_target="tpu_custom_call" | custom-call | flops 1024 | bytes 1024 | tf_op jit(solution)/shard_map/pallas_call | solution.py:336
  165.7 2.2 collective-permute-start.20
  168.0 1.1 collective-permute-start.21
  169.1 0.4 copy.13.refs_8_.refs_4_
  169.5 1.0 collective-permute-start.24
  170.5 2.3 collective-permute-start.25
  172.8 14.0 %shard_map.91.refs_6_.refs_2_ = bf16[1024,896]{1,0:T(8,128)(2,1)} custom-call(s32[64]{0:T(128)} %concatenate.36.s, bf16[1024,640]{1,0:T(8,128)(2,1)} %get-tuple-element.66.refs_0_, bf16[1024,640]{1,0:T(8,128)(2,1)} %copy-done.10, bf16[1024,640]{1,0:T(8,128)(2,1)} %copy-done.11, bf16[1024,640]{1,0:T(8,128)(2,1)} %collective-permute-done.refs_3_, ...), custom_call_target="tpu_custom_call" | custom-call | flops 1024 | bytes 1024 | tf_op jit(solution)/shard_map/pallas_call | solution.py:336
  186.9 3.2 %collective-permute-start.23 = (bf16[256,896]{1,0:T(8,128)(2,1)S(1)}, bf16[256,896]{1,0:T(8,128)(2,1)}, u32[]{:S(2)}, u32[]{:S(2)}) collective-permute-start(bf16[256,896]{1,0:T(8,128)(2,1)S(1)} %collective-permute-done.21.refs_5_), channel_id=1, source_target_pairs={{0,96},{1,97},{4,100},{5,101},{8,104},{9,105},{12,108},{13,109},{1... | collective-permute-start | bytes 1376264 | tf_op jit(solution)/shard_map/ppermute | solution.py:58
  190.2 1.2 collective-permute-done.25.refs_4_
  191.4 0.8 copy-done.8
  192.2 2.2 copy-done.2
  194.4 1.5 copy-done.4
  195.9 1.0 copy-done.9
  196.9 7.5 %shard_map.92.refs_6_ = f32[32,8]{1,0:T(8,128)S(1)} custom-call(s32[2]{0:T(128)S(1)} %pad_add_fusion.7.s, bf16[256,896]{1,0:T(8,128)(2,1)S(1)} %copy-done.6, bf16[256,896]{1,0:T(8,128)(2,1)S(1)} %copy-done.7, bf16[256,896]{1,0:T(8,128)(2,1)S(1)} %collective-permute-done.20.refs_2_, bf16[256,896]{1,0:T(8,128)(2,1)S(1)} %collective-permute-done.24.refs_3_, ...), custom_call_target="tpu_custom_call" | custom-call | flops 1024 | bytes 1024 | tf_op jit(solution)/shard_map/pallas_call | solution.py:459
  204.5 4.2 %shard_map.93 = f32[32,8]{1,0:T(8,128)S(1)} custom-call(s32[2]{0:T(128)S(1)} %pad_add_fusion.7.s, bf16[256,896]{1,0:T(8,128)(2,1)} %collective-permute-done.22.refs_0_, bf16[256,896]{1,0:T(8,128)(2,1)} %collective-permute-done.23.refs_1_, bf16[1024,896]{1,0:T(8,128)(2,1)S(1)} %copy-done.5, bf16[4,4,2,2,4,16,512]{6,5,4,3,2,1,0:T(8,128)(2,1)S(1)} %bitcast.41, ...), custom_call_target="tpu_custom_call" | custom-call | flops 1024 | bytes 1024 | tf_op jit(solution)/shard_map/pallas_call | solution.py:459
  208.8 1.2 collective-permute-done.26
  210.0 3.7 %collective-permute-done.27 = f32[32,8]{1,0:T(8,128)S(1)} collective-permute-done((f32[32,8]{1,0:T(8,128)S(1)}, f32[32,8]{1,0:T(8,128)S(1)}, u32[]{:S(2)}, u32[]{:S(2)}) %collective-permute-start.27) | collective-permute-done | bytes 1056 | tf_op jit(solution)/shard_map/ppermute | solution.py:58
  213.7 0.8 collective-permute-start.28
  214.5 4.2 %collective-permute-done.28 = f32[32,8]{1,0:T(8,128)S(1)} collective-permute-done((f32[32,8]{1,0:T(8,128)S(1)}, f32[32,8]{1,0:T(8,128)S(1)}, u32[]{:S(2)}, u32[]{:S(2)}) %collective-permute-start.28) | collective-permute-done | bytes 1056 | tf_op jit(solution)/shard_map/ppermute | solution.py:58
  218.7 1.2 collective-permute-start.29
  219.9 2.5 %collective-permute-done.29 = f32[32,8]{1,0:T(8,128)S(1)} collective-permute-done((f32[32,8]{1,0:T(8,128)S(1)}, f32[32,8]{1,0:T(8,128)S(1)}, u32[]{:S(2)}, u32[]{:S(2)}) %collective-permute-start.29) | collective-permute-done | bytes 1056 | tf_op jit(solution)/shard_map/ppermute | solution.py:58
  222.4 2.6 %collective-permute-start.30 = (f32[32,8]{1,0:T(8,128)S(1)}, f32[32,8]{1,0:T(8,128)S(1)}, u32[]{:S(2)}, u32[]{:S(2)}) collective-permute-start(f32[32,8]{1,0:T(8,128)S(1)} %add.393), channel_id=1, source_target_pairs={{0,18},{1,19},{4,22},{5,23},{8,26},{9,27},{12,30},{13,31},{16,2},{... | collective-permute-start | bytes 3080 | tf_op jit(solution)/shard_map/ppermute | solution.py:58
  225.0 2.4 %collective-permute-done.30 = f32[32,8]{1,0:T(8,128)S(1)} collective-permute-done((f32[32,8]{1,0:T(8,128)S(1)}, f32[32,8]{1,0:T(8,128)S(1)}, u32[]{:S(2)}, u32[]{:S(2)}) %collective-permute-start.30) | collective-permute-done | bytes 1056 | tf_op jit(solution)/shard_map/ppermute | solution.py:58
  227.5 0.7 copy.14
  (94 shorter events, 1.7 us)
Async XLA Ops:
  6.5 18.9 %copy-start = (s32[8,256]{1,0:T(8,128)S(1)}, s32[8,256]{1,0:T(8,128)}, u32[]{:S(2)}) copy-start(s32[8,256]{1,0:T(8,128)} %param.15) | copy-start | bytes 24580
  6.5 66.2 %all-gather.4.cloned.1.call-start = ((), (), s32[]{:S(2)}) async-start(), calls=%async_computation | async-start | bytes 3932160 | tf_op jit(solution)/shard_map/all_gather | solution.py:514
  12.7 113.2 %all-gather.6.cloned.1.call-start = ((), (), s32[]{:S(2)}) async-start(), calls=%async_computation.1 | async-start | bytes 2621440 | tf_op jit(solution)/shard_map/all_gather | solution.py:525
  12.8 50.4 %collective-permute-start.2 = (bf16[1024,640]{1,0:T(8,128)(2,1)}, bf16[1024,640]{1,0:T(8,128)(2,1)S(1)}, u32[]{:S(2)}, u32[]{:S(2)}) collective-permute-start(bf16[1024,640]{1,0:T(8,128)(2,1)} %get-tuple-element.66.refs_0_), channel_id=1, source_target_pairs={{0,32},{1,33},{4,36},{5,37},{8,40},{9,41},{12,44},{13,45},{16,48},... | collective-permute-start | bytes 3932168 | tf_op jit(solution)/shard_map/ppermute | solution.py:58
  14.8 50.6 %collective-permute-start.3 = (bf16[1024,640]{1,0:T(8,128)(2,1)}, bf16[1024,640]{1,0:T(8,128)(2,1)S(1)}, u32[]{:S(2)}, u32[]{:S(2)}) collective-permute-start(bf16[1024,640]{1,0:T(8,128)(2,1)} %get-tuple-element.66.refs_0_), channel_id=1, source_target_pairs={{0,96},{1,97},{4,100},{5,101},{8,104},{9,105},{12,108},{13,109},{1... | collective-permute-start | bytes 3932168 | tf_op jit(solution)/shard_map/ppermute | solution.py:58
  17.1 48.4 %collective-permute-start.1 = (bf16[768,1024]{1,0:T(8,128)(2,1)}, bf16[768,1024]{1,0:T(8,128)(2,1)}, u32[]{:S(2)}, u32[]{:S(2)}) collective-permute-start(bf16[768,1024]{1,0:T(8,128)(2,1)} %get-tuple-element.65), channel_id=1, source_target_pairs={{0,18},{1,19},{4,22},{5,23},{8,26},{9,27},{12,30},{13,31},{16,2},{... | collective-permute-start | bytes 4718600 | tf_op jit(solution)/shard_map/ppermute | solution.py:58
  20.1 41.4 %collective-permute-start = (bf16[1024,640]{1,0:T(8,128)(2,1)}, bf16[1024,640]{1,0:T(8,128)(2,1)}, u32[]{:S(2)}, u32[]{:S(2)}) collective-permute-start(bf16[1024,640]{1,0:T(8,128)(2,1)} %get-tuple-element.64), channel_id=1, source_target_pairs={{0,16},{1,17},{4,20},{5,21},{8,24},{9,25},{12,28},{13,29},{16,0},{... | collective-permute-start | bytes 3932168 | tf_op jit(solution)/shard_map/ppermute | solution.py:58
  20.2 41.3 %collective-permute-start.4 = (bf16[1024,256]{1,0:T(8,128)(2,1)}, bf16[1024,256]{1,0:T(8,128)(2,1)S(1)}, u32[]{:S(2)}, u32[]{:S(2)}) collective-permute-start(bf16[1024,256]{1,0:T(8,128)(2,1)} %get-tuple-element.67), channel_id=1, source_target_pairs={{0,16},{1,17},{4,20},{5,21},{8,24},{9,25},{12,28},{13,29},{16,0},{... | collective-permute-start | bytes 1572872 | tf_op jit(solution)/shard_map/ppermute | solution.py:58
  61.5 4.0 %copy-start.18 = (bf16[1024,256]{1,0:T(8,128)(2,1)}, bf16[1024,256]{1,0:T(8,128)(2,1)S(1)}, u32[]{:S(2)}) copy-start(bf16[1024,256]{1,0:T(8,128)(2,1)S(1)} %collective-permute-done.4) | copy-start | bytes 1572868
  63.2 11.8 %copy-start.10 = (bf16[1024,640]{1,0:T(8,128)(2,1)}, bf16[1024,640]{1,0:T(8,128)(2,1)S(1)}, u32[]{:S(2)}) copy-start(bf16[1024,640]{1,0:T(8,128)(2,1)S(1)} %collective-permute-done.2.refs_1_.below) | copy-start | bytes 3932164
  65.5 9.5 %copy-start.11 = (bf16[1024,640]{1,0:T(8,128)(2,1)}, bf16[1024,640]{1,0:T(8,128)(2,1)S(1)}, u32[]{:S(2)}) copy-start(bf16[1024,640]{1,0:T(8,128)(2,1)S(1)} %collective-permute-done.3.refs_2_.above) | copy-start | bytes 3932164
  65.5 126.7 %all-gather.8.cloned.1.call-start = ((), (), s32[]{:S(2)}) async-start(), calls=%async_computation.2 | async-start | bytes 4325376 | tf_op jit(solution)/shard_map/all_gather | solution.py:551
  65.5 48.4 %collective-permute-start.7 = (bf16[768,1024]{1,0:T(8,128)(2,1)}, bf16[768,1024]{1,0:T(8,128)(2,1)}, u32[]{:S(2)}, u32[]{:S(2)}) collective-permute-start(bf16[768,1024]{1,0:T(8,128)(2,1)} %collective-permute-done.1.refs_10_.refs_12_), channel_id=1, source_target_pairs={{0,4},{1,5},{4,8},{5,9},{8,12},{9,13},{12,0},{13,1},{16,20},{17,21... | collective-permute-start | bytes 4718600 | tf_op jit(solution)/shard_map/ppermute | solution.py:58
  66.9 47.1 %collective-permute-start.8 = (bf16[768,1024]{1,0:T(8,128)(2,1)}, bf16[768,1024]{1,0:T(8,128)(2,1)}, u32[]{:S(2)}, u32[]{:S(2)}) collective-permute-start(bf16[768,1024]{1,0:T(8,128)(2,1)} %collective-permute-done.1.refs_10_.refs_12_), channel_id=1, source_target_pairs={{0,12},{1,13},{4,0},{5,1},{8,4},{9,5},{12,8},{13,9},{16,28},{17,29... | collective-permute-start | bytes 4718600 | tf_op jit(solution)/shard_map/ppermute | solution.py:58
  68.8 42.9 %collective-permute-start.5 = (bf16[1024,640]{1,0:T(8,128)(2,1)}, bf16[1024,640]{1,0:T(8,128)(2,1)}, u32[]{:S(2)}, u32[]{:S(2)}) collective-permute-start(bf16[1024,640]{1,0:T(8,128)(2,1)} %collective-permute-done.refs_3_), channel_id=1, source_target_pairs={{0,32},{1,33},{4,36},{5,37},{8,40},{9,41},{12,44},{13,45},{16,48},... | collective-permute-start | bytes 3932168 | tf_op jit(solution)/shard_map/ppermute | solution.py:58
  69.1 44.8 %collective-permute-start.6 = (bf16[1024,640]{1,0:T(8,128)(2,1)}, bf16[1024,640]{1,0:T(8,128)(2,1)}, u32[]{:S(2)}, u32[]{:S(2)}) collective-permute-start(bf16[1024,640]{1,0:T(8,128)(2,1)} %collective-permute-done.refs_3_), channel_id=1, source_target_pairs={{0,96},{1,97},{4,100},{5,101},{8,104},{9,105},{12,108},{13,109},{1... | collective-permute-start | bytes 3932168 | tf_op jit(solution)/shard_map/ppermute | solution.py:58
  75.0 25.3 %collective-permute-start.9 = (bf16[64,8192]{1,0:T(8,128)(2,1)}, bf16[64,8192]{1,0:T(8,128)(2,1)S(1)}, u32[]{:S(2)}, u32[]{:S(2)}) collective-permute-start(bf16[64,8192]{1,0:T(8,128)(2,1)} %shard_map.85.mine), channel_id=1, source_target_pairs={{0,16},{1,17},{4,20},{5,21},{8,24},{9,25},{12,28},{13,29},{16,0},{... | collective-permute-start | bytes 3145736 | tf_op jit(solution)/shard_map/ppermute | solution.py:58
  100.3 1.0 copy-start.17
  114.0 7.4 %collective-permute-start.10 = (bf16[768,1024]{1,0:T(8,128)(2,1)}, bf16[768,1024]{1,0:T(8,128)(2,1)S(1)}, u32[]{:S(2)}, u32[]{:S(2)}) collective-permute-start(bf16[768,1024]{1,0:T(8,128)(2,1)} %collective-permute-done.1.refs_10_.refs_12_), channel_id=1, source_target_pairs={{0,1},{1,0},{4,5},{5,4},{8,9},{9,8},{12,13},{13,12},{16,17},{17,16... | collective-permute-start | bytes 4718600 | tf_op jit(solution)/shard_map/ppermute | solution.py:58
  114.1 8.6 %collective-permute-start.11 = (bf16[768,1024]{1,0:T(8,128)(2,1)}, bf16[768,1024]{1,0:T(8,128)(2,1)}, u32[]{:S(2)}, u32[]{:S(2)}) collective-permute-start(bf16[768,1024]{1,0:T(8,128)(2,1)} %collective-permute-done.7.x_below.refs_12_.refs_14_), channel_id=1, source_target_pairs={{0,1},{1,0},{4,5},{5,4},{8,9},{9,8},{12,13},{13,12},{16,17},{17,16... | collective-permute-start | bytes 4718600 | tf_op jit(solution)/shard_map/ppermute | solution.py:58
  114.6 8.1 %collective-permute-start.12 = (bf16[768,1024]{1,0:T(8,128)(2,1)}, bf16[768,1024]{1,0:T(8,128)(2,1)}, u32[]{:S(2)}, u32[]{:S(2)}) collective-permute-start(bf16[768,1024]{1,0:T(8,128)(2,1)} %collective-permute-done.8.x_above.refs_14_.refs_16_), channel_id=1, source_target_pairs={{0,1},{1,0},{4,5},{5,4},{8,9},{9,8},{12,13},{13,12},{16,17},{17,16... | collective-permute-start | bytes 4718600 | tf_op jit(solution)/shard_map/ppermute | solution.py:58
  117.6 33.4 %collective-permute-start.15 = (bf16[1024,640]{1,0:T(8,128)(2,1)}, bf16[1024,640]{1,0:T(8,128)(2,1)}, u32[]{:S(2)}, u32[]{:S(2)}) collective-permute-start(bf16[1024,640]{1,0:T(8,128)(2,1)} %bitcast.43), channel_id=1, source_target_pairs={{0,32},{1,33},{4,36},{5,37},{8,40},{9,41},{12,44},{13,45},{16,48},... | collective-permute-start | bytes 3932168 | tf_op jit(solution)/shard_map/ppermute | solution.py:58
  117.7 33.3 %collective-permute-start.16 = (bf16[1024,640]{1,0:T(8,128)(2,1)}, bf16[1024,640]{1,0:T(8,128)(2,1)}, u32[]{:S(2)}, u32[]{:S(2)}) collective-permute-start(bf16[1024,640]{1,0:T(8,128)(2,1)} %bitcast.44), channel_id=1, source_target_pairs={{0,96},{1,97},{4,100},{5,101},{8,104},{9,105},{12,108},{13,109},{1... | collective-permute-start | bytes 3932168 | tf_op jit(solution)/shard_map/ppermute | solution.py:58
  121.4 4.5 %copy-start.12 = (bf16[768,1024]{1,0:T(8,128)(2,1)}, bf16[768,1024]{1,0:T(8,128)(2,1)S(1)}, u32[]{:S(2)}) copy-start(bf16[768,1024]{1,0:T(8,128)(2,1)S(1)} %collective-permute-done.10.refs_11_.refs_13_) | copy-start | bytes 4718596
  121.4 23.6 %collective-permute-start.17 = (bf16[784,512]{1,0:T(8,128)(2,1)}, bf16[784,512]{1,0:T(8,128)(2,1)S(1)}, u32[]{:S(2)}, u32[]{:S(2)}) collective-permute-start(bf16[784,512]{1,0:T(8,128)(2,1)} %get-tuple-element.103), channel_id=1, source_target_pairs={{0,16},{1,17},{4,20},{5,21},{8,24},{9,25},{12,28},{13,29},{16,0},{... | collective-permute-start | bytes 2408456 | tf_op jit(solution)/shard_map/ppermute | solution.py:58
  122.7 28.3 %collective-permute-start.13 = (bf16[384,1024]{1,0:T(8,128)(2,1)}, bf16[384,1024]{1,0:T(8,128)(2,1)S(1)}, u32[]{:S(2)}, u32[]{:S(2)}) collective-permute-start(bf16[384,1024]{1,0:T(8,128)(2,1)} %get-tuple-element.91), channel_id=1, source_target_pairs={{0,4},{1,5},{4,8},{5,9},{8,12},{9,13},{12,0},{13,1},{16,20},{17,21... | collective-permute-start | bytes 2359304 | tf_op jit(solution)/shard_map/ppermute | solution.py:58
  123.0 28.0 %collective-permute-start.14 = (bf16[384,1024]{1,0:T(8,128)(2,1)}, bf16[384,1024]{1,0:T(8,128)(2,1)}, u32[]{:S(2)}, u32[]{:S(2)}) collective-permute-start(bf16[384,1024]{1,0:T(8,128)(2,1)} %get-tuple-element.92), channel_id=1, source_target_pairs={{0,12},{1,13},{4,0},{5,1},{8,4},{9,5},{12,8},{13,9},{16,28},{17,29... | collective-permute-start | bytes 2359304 | tf_op jit(solution)/shard_map/ppermute | solution.py:58
  145.0 9.7 %copy-start.13 = (bf16[784,512]{1,0:T(8,128)(2,1)}, bf16[784,512]{1,0:T(8,128)(2,1)S(1)}, u32[]{:S(2)}) copy-start(bf16[784,512]{1,0:T(8,128)(2,1)S(1)} %collective-permute-done.17.refs_25_) | copy-start | bytes 2408452
  151.0 3.7 %copy-start.14 = (bf16[384,1024]{1,0:T(8,128)(2,1)}, bf16[384,1024]{1,0:T(8,128)(2,1)S(1)}, u32[]{:S(2)}) copy-start(bf16[384,1024]{1,0:T(8,128)(2,1)S(1)} %collective-permute-done.13.refs_18_) | copy-start | bytes 2359300
  151.0 2.6 %collective-permute-start.18 = (bf16[384,1024]{1,0:T(8,128)(2,1)S(1)}, bf16[384,1024]{1,0:T(8,128)(2,1)S(1)}, u32[]{:S(2)}, u32[]{:S(2)}) collective-permute-start(bf16[384,1024]{1,0:T(8,128)(2,1)S(1)} %collective-permute-done.13.refs_18_), channel_id=1, source_target_pairs={{0,1},{1,0},{4,5},{5,4},{8,9},{9,8},{12,13},{13,12},{16,17},{17,16... | collective-permute-start | bytes 2359304 | tf_op jit(solution)/shard_map/ppermute | solution.py:58
  151.1 3.6 %collective-permute-start.19 = (bf16[384,1024]{1,0:T(8,128)(2,1)}, bf16[384,1024]{1,0:T(8,128)(2,1)S(1)}, u32[]{:S(2)}, u32[]{:S(2)}) collective-permute-start(bf16[384,1024]{1,0:T(8,128)(2,1)} %collective-permute-done.14.refs_19_), channel_id=1, source_target_pairs={{0,1},{1,0},{4,5},{5,4},{8,9},{9,8},{12,13},{13,12},{16,17},{17,16... | collective-permute-start | bytes 2359304 | tf_op jit(solution)/shard_map/ppermute | solution.py:58
  153.6 1.2 copy-start.15
  154.7 0.9 copy-start.16
  165.7 21.0 %collective-permute-start.20 = (bf16[256,896]{1,0:T(8,128)(2,1)}, bf16[256,896]{1,0:T(8,128)(2,1)S(1)}, u32[]{:S(2)}, u32[]{:S(2)}) collective-permute-start(bf16[256,896]{1,0:T(8,128)(2,1)} %get-tuple-element.114.refs_0_), channel_id=1, source_target_pairs={{0,32},{1,33},{4,36},{5,37},{8,40},{9,41},{12,44},{13,45},{16,48},... | collective-permute-start | bytes 1376264 | tf_op jit(solution)/shard_map/ppermute | solution.py:58
  168.0 18.8 %collective-permute-start.21 = (bf16[256,896]{1,0:T(8,128)(2,1)}, bf16[256,896]{1,0:T(8,128)(2,1)S(1)}, u32[]{:S(2)}, u32[]{:S(2)}) collective-permute-start(bf16[256,896]{1,0:T(8,128)(2,1)} %get-tuple-element.115.refs_1_), channel_id=1, source_target_pairs={{0,96},{1,97},{4,100},{5,101},{8,104},{9,105},{12,108},{13,109},{1... | collective-permute-start | bytes 1376264 | tf_op jit(solution)/shard_map/ppermute | solution.py:58
  169.4 20.7 %copy-start.19 = (s32[1,512]{1,0:T(1,128)S(1)}, s32[1,512]{1,0:T(1,128)}, u32[]{:S(2)}) copy-start(s32[1,512]{1,0:T(1,128)} %ids.1) | copy-start | bytes 6148
  169.4 22.8 %copy-start.6 = (bf16[256,896]{1,0:T(8,128)(2,1)S(1)}, bf16[256,896]{1,0:T(8,128)(2,1)}, u32[]{:S(2)}) copy-start(bf16[256,896]{1,0:T(8,128)(2,1)} %get-tuple-element.114.refs_0_) | copy-start | bytes 1376260
  169.4 22.8 %copy-start.7 = (bf16[256,896]{1,0:T(8,128)(2,1)S(1)}, bf16[256,896]{1,0:T(8,128)(2,1)}, u32[]{:S(2)}) copy-start(bf16[256,896]{1,0:T(8,128)(2,1)} %get-tuple-element.115.refs_1_) | copy-start | bytes 1376260
  169.5 20.7 %collective-permute-start.24 = (bf16[256,896]{1,0:T(8,128)(2,1)}, bf16[256,896]{1,0:T(8,128)(2,1)S(1)}, u32[]{:S(2)}, u32[]{:S(2)}) collective-permute-start(bf16[256,896]{1,0:T(8,128)(2,1)} %get-tuple-element.115.refs_1_), channel_id=1, source_target_pairs={{0,32},{1,33},{4,36},{5,37},{8,40},{9,41},{12,44},{13,45},{16,48},... | collective-permute-start | bytes 1376264 | tf_op jit(solution)/shard_map/ppermute | solution.py:58
  170.5 20.9 %collective-permute-start.25 = (bf16[256,896]{1,0:T(8,128)(2,1)}, bf16[256,896]{1,0:T(8,128)(2,1)S(1)}, u32[]{:S(2)}, u32[]{:S(2)}) collective-permute-start(bf16[256,896]{1,0:T(8,128)(2,1)} %get-tuple-element.114.refs_0_), channel_id=1, source_target_pairs={{0,96},{1,97},{4,100},{5,101},{8,104},{9,105},{12,108},{13,109},{1... | collective-permute-start | bytes 1376264 | tf_op jit(solution)/shard_map/ppermute | solution.py:58
  186.8 17.7 %collective-permute-start.22 = (bf16[256,896]{1,0:T(8,128)(2,1)S(1)}, bf16[256,896]{1,0:T(8,128)(2,1)}, u32[]{:S(2)}, u32[]{:S(2)}) collective-permute-start(bf16[256,896]{1,0:T(8,128)(2,1)S(1)} %collective-permute-done.20.refs_2_), channel_id=1, source_target_pairs={{0,32},{1,33},{4,36},{5,37},{8,40},{9,41},{12,44},{13,45},{16,48},... | collective-permute-start | bytes 1376264 | tf_op jit(solution)/shard_map/ppermute | solution.py:58
  186.9 17.6 %collective-permute-start.23 = (bf16[256,896]{1,0:T(8,128)(2,1)S(1)}, bf16[256,896]{1,0:T(8,128)(2,1)}, u32[]{:S(2)}, u32[]{:S(2)}) collective-permute-start(bf16[256,896]{1,0:T(8,128)(2,1)S(1)} %collective-permute-done.21.refs_5_), channel_id=1, source_target_pairs={{0,96},{1,97},{4,100},{5,101},{8,104},{9,105},{12,108},{13,109},{1... | collective-permute-start | bytes 1376264 | tf_op jit(solution)/shard_map/ppermute | solution.py:58
  191.4 0.8 copy-start.8
  192.2 2.2 copy-start.2
  194.4 1.5 copy-start.4
  195.9 1.0 copy-start.9
  196.9 7.6 %copy-start.3 = (bf16[4096,512]{1,0:T(8,128)(2,1)S(1)}, bf16[4096,512]{1,0:T(8,128)(2,1)}, u32[]{:S(2)}) copy-start(bf16[4096,512]{1,0:T(8,128)(2,1)} %all-gather.8.cloned.1.call-done) | copy-start | bytes 12582916
  196.9 7.6 %copy-start.5 = (bf16[1024,896]{1,0:T(8,128)(2,1)S(1)}, bf16[1024,896]{1,0:T(8,128)(2,1)}, u32[]{:S(2)}) copy-start(bf16[1024,896]{1,0:T(8,128)(2,1)} %shard_map.91.refs_6_.refs_2_) | copy-start | bytes 5505028
  204.5 23.6 %copy-start.1 = (s32[8,256]{1,0:T(8,128)S(1)}, s32[8,256]{1,0:T(8,128)}, u32[]{:S(2)}) copy-start(s32[8,256]{1,0:T(8,128)} %param.15) | copy-start | bytes 24580
  208.7 1.3 collective-permute-start.26
  210.0 3.7 %collective-permute-start.27 = (f32[32,8]{1,0:T(8,128)S(1)}, f32[32,8]{1,0:T(8,128)S(1)}, u32[]{:S(2)}, u32[]{:S(2)}) collective-permute-start(f32[32,8]{1,0:T(8,128)S(1)} %add.390), channel_id=1, source_target_pairs={{0,4},{1,5},{4,0},{5,1},{8,12},{9,13},{12,8},{13,9},{16,20},{17,21... | collective-permute-start | bytes 3080 | tf_op jit(solution)/shard_map/ppermute | solution.py:58
  213.7 4.9 %collective-permute-start.28 = (f32[32,8]{1,0:T(8,128)S(1)}, f32[32,8]{1,0:T(8,128)S(1)}, u32[]{:S(2)}, u32[]{:S(2)}) collective-permute-start(f32[32,8]{1,0:T(8,128)S(1)} %add.391), channel_id=1, source_target_pairs={{0,12},{1,13},{4,8},{5,9},{8,4},{9,5},{12,0},{13,1},{16,28},{17,29... | collective-permute-start | bytes 3080 | tf_op jit(solution)/shard_map/ppermute | solution.py:58
  218.7 3.7 %collective-permute-start.29 = (f32[32,8]{1,0:T(8,128)S(1)}, f32[32,8]{1,0:T(8,128)S(1)}, u32[]{:S(2)}, u32[]{:S(2)}) collective-permute-start(f32[32,8]{1,0:T(8,128)S(1)} %add.392), channel_id=1, source_target_pairs={{0,16},{1,17},{4,20},{5,21},{8,24},{9,25},{12,28},{13,29},{16,0},{... | collective-permute-start | bytes 3080 | tf_op jit(solution)/shard_map/ppermute | solution.py:58
  222.4 4.9 %collective-permute-start.30 = (f32[32,8]{1,0:T(8,128)S(1)}, f32[32,8]{1,0:T(8,128)S(1)}, u32[]{:S(2)}, u32[]{:S(2)}) collective-permute-start(f32[32,8]{1,0:T(8,128)S(1)} %add.393), channel_id=1, source_target_pairs={{0,18},{1,19},{4,22},{5,23},{8,26},{9,27},{12,30},{13,31},{16,2},{... | collective-permute-start | bytes 3080 | tf_op jit(solution)/shard_map/ppermute | solution.py:58
Sparse Core Ops, SparseCore 0:
  12.8 59.8 all-gather.3
  74.4 42.1 all-gather.5
  118.8 48.3 all-gather.7
